TPU v7x, 256 devices: a whole 4x4x8 slice. The times are simulated.
256 devices in a mesh: tm: 8 (over z_lo, core), tile: 32 (over y, z_hi, x).
Axes of the slice: x: 4, y: 4, z: 8 (z_hi: 2, z_lo: 4; z = z_hi * 4 + z_lo), core: 2. Of those that a mesh axis runs over, the one named last changes fastest.
Arguments:
- initial_states: float32 [8, 128, 64, 256], P('tm', 'tile'), may hold values from 0 to 2
- material: int32 [128, 64, 256], P('tile'), may hold values from 0 to 11
- conductivity: float32 [12], replicated, may hold values from 0.3 to 1
- dispersivity: float32 [12], replicated, may hold values from 0.01 to 0.03
- freundlich_k: float32 [12], replicated, may hold values from 0.1 to 1
- freundlich_n: float32 [12], replicated, may hold values from 0.5 to 0.95
- surface_load: float32 [128, 64], P('tile'), may hold values from 0 to 1.5
Outputs:
- end_states: float32 [8, 128, 64, 256], P('tm', 'tile')
All inputs are finite; a program needn't handle non-finite values.
Results may differ from a plain program's by a relative error of at most 0.0001.
Values sent between devices are 32-bit elements; how exact they have to be, the bound alone decides.
A program may use at most 128 MiB of HBM per device.

v0:
```python
import jax
import jax.numpy as jnp
from jax import lax
from jax.sharding import PartitionSpec as P

STEPS = 4
COARSE_STEPS = 2


def padded_2(block, sides, width):
    for axis, dim in sides:
        count = lax.axis_size(axis)
        forward = [(i, i + 1) for i in range(count - 1)]
        backward = [(target, source) for source, target in forward]
        low = lax.ppermute(
            lax.slice_in_dim(block, block.shape[dim] - width, None, axis=dim), axis, forward
        )
        high = lax.ppermute(lax.slice_in_dim(block, 0, width, axis=dim), axis, backward)
        block = jnp.concatenate([low, block, high], axis=dim)
    return block


def from_behind(block, axis, distance):
    devices = range(lax.axis_size(axis))
    route = [(i - distance, i) for i in devices if i - distance in devices]
    return lax.ppermute(block, axis, route)


def lookup(material, table):
    result = jnp.zeros(material.shape, jnp.float32)
    for material_id in range(table.shape[0]):
        result = jnp.where(material == material_id, table[material_id], result)
    return result


def coefficients(material, conductivity, dispersivity, freundlich_k, freundlich_n, surface_load):
    cond = lookup(material, conductivity)
    drift_x = 0.5 * cond
    drift_z = 0.3 * cond
    spread = lookup(material, dispersivity) * cond
    sorb_k = lookup(material, freundlich_k)
    sorb_n = lookup(material, freundlich_n)
    inflow = jnp.zeros(material.shape, jnp.float32).at[:, :, 0].set(surface_load)
    return (drift_x, drift_z, spread, sorb_k, sorb_n, inflow)


def advance(padded, coefs, spacing, time_step):
    drift_x, drift_z, spread, sorb_k, sorb_n, inflow = coefs
    middle = padded[1:-1]
    behind = padded[:-2]
    ahead = padded[2:]
    padded_yz = jnp.pad(middle, ((0, 0), (1, 1), (1, 1)))
    upper_cell = padded_yz[:, 1:-1, :-2]
    neighbours = (
        behind
        + ahead
        + padded_yz[:, 2:, 1:-1]
        + padded_yz[:, :-2, 1:-1]
        + padded_yz[:, 1:-1, 2:]
        + upper_cell
    )
    change = (
        spread / (spacing * spacing) * (neighbours - 6.0 * middle)
        - drift_x / spacing * (middle - behind)
        - drift_z / spacing * (middle - upper_cell)
        + inflow
    )
    retardation = 1.0 + sorb_k * sorb_n * (jnp.abs(middle) + 1.0) ** (sorb_n - 1.0)
    return middle + time_step * change / retardation


def coarsen(field):
    first, second, third = field.shape
    return field.reshape(first // 2, 2, second // 2, 2, third // 2, 2).mean(axis=(1, 3, 5))


def refine(field):
    return jnp.repeat(jnp.repeat(jnp.repeat(field, 2, axis=0), 2, axis=1), 2, axis=2)


def coarse_run(state, coefs):
    for repeat in range(COARSE_STEPS):
        padded = padded_2(state, (("tile", 0),), 1)
        state = advance(padded, coefs, 2.0, 2.0)
    return state


def shards(
    initial_states, material, conductivity, dispersivity, freundlich_k, freundlich_n, surface_load
):
    own = initial_states[0]
    coefs = coefficients(
        material, conductivity, dispersivity, freundlich_k, freundlich_n, surface_load
    )
    state = own
    for repeat in range(STEPS):
        padded = padded_2(state, (("tile", 0),), 1)
        state = advance(padded, coefs, 1.0, 1.0)
    coarse_coefs = tuple((coarsen(field) for field in coefs))
    start_own = coarsen(own)
    coarse_now = coarse_run(start_own, coarse_coefs)
    delta = state - refine(coarse_now)
    coarse_delta = coarsen(delta)
    leading = lax.axis_index("tm") == 0
    for repeat in range(lax.axis_size("tm") - 1):
        arrived = from_behind(coarse_now + coarse_delta, "tm", 1)
        start = jnp.where(leading, start_own, arrived)
        coarse_now = coarse_run(start, coarse_coefs)
    return (refine(coarse_now) + delta)[None]


def solution(mesh):
    in_specs = (
        P("tm", "tile", None, None),
        P("tile", None, None),
        P(),
        P(),
        P(),
        P(),
        P("tile", None),
    )
    out_specs = P("tm", "tile", None, None)
    return jax.shard_map(shards, mesh=mesh, in_specs=in_specs, out_specs=out_specs, check_vma=False)
```

profile of v0, /device:TPU:89, one launch (start us, length us, event | category | flops | bytes accessed | tf_op | source)
XLA Modules:
  0.0 575.9 jit_solution(4311793074646980032)
XLA Ops:
  0.9 9.4 %collective-permute-start.5 = (f32[1,64,256]{2,1,0:T(8,128)S(1)}, f32[1,64,256]{2,1,0:T(8,128)S(1)}, u32[]{:S(2)}, u32[]{:S(2)}) collective-permute-start(f32[1,64,256]{2,1,0:T(8,128)S(1)} %get-tuple-element.48), channel_id=1, source_target_pairs={{1,0},{2,1},{3,2},{4,3},{5,4},{6,5},{7,6},{8,7},{9,8},{10,9},{11,1... | collective-permute-start | bytes 196616 | tf_op jit(solution)/shard_map/ppermute | solution.py:18
  22.2 17.8 %fusion.7 = (f32[4,64,256]{2,1,0:T(8,128)S(1)}, f32[4,64,256]{2,1,0:T(8,128)S(1)}, f32[4,64,256]{2,1,0:T(8,128)S(1)}, pred[4,64,256]{2,1,0:T(8,128)(4,1)S(1)}, p...) fusion(f32[4,64,256]{2,1,0:T(8,128)} %bitcast.65, ...), kind=kLoop, calls=%fused_computation.23 | loop fusion | flops 3604480 | bytes 2228320 | tf_op jit(solution)/shard_map/sub | solution.py:63
  40.2 16.7 %divide_add_fusion.2 = (f32[4,64,256]{2,1,0:T(8,128)S(1)}, f32[4,64,256]{2,1,0:T(8,128)S(1)}, f32[4,64,256]{2,1,0:T(8,128)S(1)}, f32[4,64,256]{2,1,0:T(8,128)S(1)}) fusion(f32[4,64,256]{2,1,0:T(8,128)S(1)} %add.637, f32[1,4,64,256]{3,2,1,0:T(8,128)} %param.9, pred[4,64,256]{2,1,0:T(8,128)(4,1)S(1)} %get-tuple-element.35, ...), kind=kLoop, calls=%fused_computation.72 | loop fusion | flops 2097152 | bytes 2359392 | tf_op jit(solution)/shard_map/add | solution.py:69
  57.0 8.3 %collective-permute-start.7 = (f32[1,64,256]{2,1,0:T(8,128)S(1)}, f32[1,64,256]{2,1,0:T(8,128)S(1)}, u32[]{:S(2)}, u32[]{:S(2)}) collective-permute-start(f32[1,64,256]{2,1,0:T(8,128)S(1)} %get-tuple-element.46), channel_id=1, source_target_pairs={{1,0},{2,1},{3,2},{4,3},{5,4},{6,5},{7,6},{8,7},{9,8},{10,9},{11,1... | collective-permute-start | bytes 196616 | tf_op jit(solution)/shard_map/ppermute | solution.py:18
  67.2 18.8 %reshape_squeeze.3 = f32[2,2,32,2,128,2]{5,4,3,2,1,0:T(8,128)} reshape(f32[1,4,64,256]{3,2,1,0:T(8,128)} %param.9) | data formatting | bytes 524288 | tf_op jit(solution)/shard_map/reshape;squeeze | solution.py:74
  94.0 10.3 %collective-permute-start.9 = (f32[1,64,256]{2,1,0:T(8,128)S(1)}, f32[1,64,256]{2,1,0:T(8,128)S(1)}, u32[]{:S(2)}, u32[]{:S(2)}) collective-permute-start(f32[1,64,256]{2,1,0:T(8,128)S(1)} %get-tuple-element.44), channel_id=1, source_target_pairs={{1,0},{2,1},{3,2},{4,3},{5,4},{6,5},{7,6},{8,7},{9,8},{10,9},{11,1... | collective-permute-start | bytes 196616 | tf_op jit(solution)/shard_map/ppermute | solution.py:18
  106.2 10.0 %collective-permute-done.8 = f32[1,64,256]{2,1,0:T(8,128)S(1)} collective-permute-done((f32[1,64,256]{2,1,0:T(8,128)S(1)}, f32[1,64,256]{2,1,0:T(8,128)S(1)}, u32[]{:S(2)}, u32[]{:S(2)}) %collective-permute-start.8) | collective-permute-done | bytes 65568 | tf_op jit(solution)/shard_map/ppermute | solution.py:15
  122.5 8.8 %collective-permute-start.1 = (f32[1,32,128]{2,1,0:T(8,128)S(1)}, f32[1,32,128]{2,1,0:T(8,128)S(1)}, u32[]{:S(2)}, u32[]{:S(2)}) collective-permute-start(f32[1,32,128]{2,1,0:T(8,128)S(1)} %get-tuple-element.80), channel_id=1, source_target_pairs={{1,0},{2,1},{3,2},{4,3},{5,4},{6,5},{7,6},{8,7},{9,8},{10,9},{11,1... | collective-permute-start | bytes 49160 | tf_op jit(solution)/shard_map/ppermute | solution.py:18
  133.5 18.1 %reshape.79 = f32[2,2,32,2,128,2]{5,4,3,2,1,0:T(8,128)} reshape(f32[4,64,256]{2,1,0:T(8,128)S(1)} %scatter.13.clone) | data formatting | bytes 524288 | tf_op jit(solution)/shard_map/reshape | solution.py:74
  158.5 18.1 %reshape.75 = f32[2,2,32,2,128,2]{5,4,3,2,1,0:T(8,128)} reshape(f32[4,64,256]{2,1,0:T(8,128)S(1)} %get-tuple-element.22) | data formatting | bytes 524288 | tf_op jit(solution)/shard_map/reshape | solution.py:74
  176.6 18.1 %reshape.81 = f32[2,2,32,2,128,2]{5,4,3,2,1,0:T(8,128)} reshape(f32[4,64,256]{2,1,0:T(8,128)S(1)} %get-tuple-element.19) | data formatting | bytes 524288 | tf_op jit(solution)/shard_map/reshape | solution.py:74
  208.6 18.1 %reshape.80 = f32[2,2,32,2,128,2]{5,4,3,2,1,0:T(8,128)} reshape(f32[4,64,256]{2,1,0:T(8,128)S(1)} %get-tuple-element.20) | data formatting | bytes 524288 | tf_op jit(solution)/shard_map/reshape | solution.py:74
  233.9 18.1 %reshape.76 = f32[2,2,32,2,128,2]{5,4,3,2,1,0:T(8,128)} reshape(f32[4,64,256]{2,1,0:T(8,128)S(1)} %get-tuple-element.40) | data formatting | bytes 524288 | tf_op jit(solution)/shard_map/reshape | solution.py:74
  259.0 18.1 %reshape.77 = f32[2,2,32,2,128,2]{5,4,3,2,1,0:T(8,128)} reshape(f32[4,64,256]{2,1,0:T(8,128)S(1)} %get-tuple-element.39) | data formatting | bytes 524288 | tf_op jit(solution)/shard_map/reshape | solution.py:74
  284.2 10.3 %collective-permute-start.3 = (f32[1,32,128]{2,1,0:T(8,128)S(1)}, f32[1,32,128]{2,1,0:T(8,128)S(1)}, u32[]{:S(2)}, u32[]{:S(2)}) collective-permute-start(f32[1,32,128]{2,1,0:T(8,128)S(1)} %get-tuple-element.78), channel_id=1, source_target_pairs={{1,0},{2,1},{3,2},{4,3},{5,4},{6,5},{7,6},{8,7},{9,8},{10,9},{11,1... | collective-permute-start | bytes 49160 | tf_op jit(solution)/shard_map/ppermute | solution.py:18
  296.6 9.2 %collective-permute-done.2 = f32[1,32,128]{2,1,0:T(8,128)S(1)} collective-permute-done((f32[1,32,128]{2,1,0:T(8,128)S(1)}, f32[1,32,128]{2,1,0:T(8,128)S(1)}, u32[]{:S(2)}, u32[]{:S(2)}) %collective-permute-start.2) | collective-permute-done | bytes 16416 | tf_op jit(solution)/shard_map/ppermute | solution.py:15
  307.0 18.1 %reshape.85 = f32[2,2,32,2,128,2]{5,4,3,2,1,0:T(8,128)} reshape(f32[4,64,256]{2,1,0:T(8,128)S(1)} %add_subtract_fusion) | data formatting | bytes 524288 | tf_op jit(solution)/shard_map/reshape | solution.py:74
  332.1 8.0 %collective-permute-start.12 = (f32[2,32,128]{2,1,0:T(8,128)S(1)}, f32[2,32,128]{2,1,0:T(8,128)S(1)}, u32[]{:S(2)}, u32[]{:S(2)}) collective-permute-start(f32[2,32,128]{2,1,0:T(8,128)S(1)} %multiply_add_fusion.1), channel_id=1, source_target_pairs={{0,32},{32,64},{64,96},{96,128},{128,160},{160,192},{192,224},{1,3... | collective-permute-start | bytes 98312 | tf_op jit(solution)/shard_map/ppermute | solution.py:26
  346.5 8.1 %collective-permute-done.13 = f32[1,32,128]{2,1,0:T(8,128)S(1)} collective-permute-done((f32[1,32,128]{2,1,0:T(8,128)S(1)}, f32[1,32,128]{2,1,0:T(8,128)S(1)}, u32[]{:S(2)}, u32[]{:S(2)}) %collective-permute-start.13) | collective-permute-done | bytes 16416 | tf_op jit(solution)/shard_map/ppermute | solution.py:15
  360.0 8.0 %collective-permute-done.15 = f32[1,32,128]{2,1,0:T(8,128)S(1)} collective-permute-done((f32[1,32,128]{2,1,0:T(8,128)S(1)}, f32[1,32,128]{2,1,0:T(8,128)S(1)}, u32[]{:S(2)}, u32[]{:S(2)}) %collective-permute-start.15) | collective-permute-done | bytes 16416 | tf_op jit(solution)/shard_map/ppermute | solution.py:15
  380.9 8.0 %collective-permute-done.18 = f32[1,32,128]{2,1,0:T(8,128)S(1)} collective-permute-done((f32[1,32,128]{2,1,0:T(8,128)S(1)}, f32[1,32,128]{2,1,0:T(8,128)S(1)}, u32[]{:S(2)}, u32[]{:S(2)}) %collective-permute-start.18) | collective-permute-done | bytes 16416 | tf_op jit(solution)/shard_map/ppermute | solution.py:15
  394.3 8.0 %collective-permute-done.20 = f32[1,32,128]{2,1,0:T(8,128)S(1)} collective-permute-done((f32[1,32,128]{2,1,0:T(8,128)S(1)}, f32[1,32,128]{2,1,0:T(8,128)S(1)}, u32[]{:S(2)}, u32[]{:S(2)}) %collective-permute-start.20) | collective-permute-done | bytes 16416 | tf_op jit(solution)/shard_map/ppermute | solution.py:15
  415.3 8.0 %collective-permute-done.23 = f32[1,32,128]{2,1,0:T(8,128)S(1)} collective-permute-done((f32[1,32,128]{2,1,0:T(8,128)S(1)}, f32[1,32,128]{2,1,0:T(8,128)S(1)}, u32[]{:S(2)}, u32[]{:S(2)}) %collective-permute-start.23) | collective-permute-done | bytes 16416 | tf_op jit(solution)/shard_map/ppermute | solution.py:15
  428.7 8.0 %collective-permute-done.25 = f32[1,32,128]{2,1,0:T(8,128)S(1)} collective-permute-done((f32[1,32,128]{2,1,0:T(8,128)S(1)}, f32[1,32,128]{2,1,0:T(8,128)S(1)}, u32[]{:S(2)}, u32[]{:S(2)}) %collective-permute-start.25) | collective-permute-done | bytes 16416 | tf_op jit(solution)/shard_map/ppermute | solution.py:15
  (164 shorter events, 272.6 us)
Async XLA Ops:
  0.9 19.3 %collective-permute-start.5 = (f32[1,64,256]{2,1,0:T(8,128)S(1)}, f32[1,64,256]{2,1,0:T(8,128)S(1)}, u32[]{:S(2)}, u32[]{:S(2)}) collective-permute-start(f32[1,64,256]{2,1,0:T(8,128)S(1)} %get-tuple-element.48), channel_id=1, source_target_pairs={{1,0},{2,1},{3,2},{4,3},{5,4},{6,5},{7,6},{8,7},{9,8},{10,9},{11,1... | collective-permute-start | bytes 196616 | tf_op jit(solution)/shard_map/ppermute | solution.py:18
  10.3 11.9 %collective-permute-start.4 = (f32[1,64,256]{2,1,0:T(8,128)S(1)}, f32[1,64,256]{2,1,0:T(8,128)S(1)}, u32[]{:S(2)}, u32[]{:S(2)}) collective-permute-start(f32[1,64,256]{2,1,0:T(8,128)S(1)} %get-tuple-element.47), channel_id=1, source_target_pairs={{0,1},{1,2},{2,3},{3,4},{4,5},{5,6},{6,7},{7,8},{8,9},{9,10},{10,1... | collective-permute-start | bytes 196616 | tf_op jit(solution)/shard_map/ppermute | solution.py:15
  57.0 36.0 %collective-permute-start.7 = (f32[1,64,256]{2,1,0:T(8,128)S(1)}, f32[1,64,256]{2,1,0:T(8,128)S(1)}, u32[]{:S(2)}, u32[]{:S(2)}) collective-permute-start(f32[1,64,256]{2,1,0:T(8,128)S(1)} %get-tuple-element.46), channel_id=1, source_target_pairs={{1,0},{2,1},{3,2},{4,3},{5,4},{6,5},{7,6},{8,7},{9,8},{10,9},{11,1... | collective-permute-start | bytes 196616 | tf_op jit(solution)/shard_map/ppermute | solution.py:18
  65.2 27.7 %collective-permute-start.6 = (f32[1,64,256]{2,1,0:T(8,128)S(1)}, f32[1,64,256]{2,1,0:T(8,128)S(1)}, u32[]{:S(2)}, u32[]{:S(2)}) collective-permute-start(f32[1,64,256]{2,1,0:T(8,128)S(1)} %get-tuple-element.45), channel_id=1, source_target_pairs={{0,1},{1,2},{2,3},{3,4},{4,5},{5,6},{6,7},{7,8},{8,9},{9,10},{10,1... | collective-permute-start | bytes 196616 | tf_op jit(solution)/shard_map/ppermute | solution.py:15
  94.0 12.2 %collective-permute-start.9 = (f32[1,64,256]{2,1,0:T(8,128)S(1)}, f32[1,64,256]{2,1,0:T(8,128)S(1)}, u32[]{:S(2)}, u32[]{:S(2)}) collective-permute-start(f32[1,64,256]{2,1,0:T(8,128)S(1)} %get-tuple-element.44), channel_id=1, source_target_pairs={{1,0},{2,1},{3,2},{4,3},{5,4},{6,5},{7,6},{8,7},{9,8},{10,9},{11,1... | collective-permute-start | bytes 196616 | tf_op jit(solution)/shard_map/ppermute | solution.py:18
  104.3 11.9 %collective-permute-start.8 = (f32[1,64,256]{2,1,0:T(8,128)S(1)}, f32[1,64,256]{2,1,0:T(8,128)S(1)}, u32[]{:S(2)}, u32[]{:S(2)}) collective-permute-start(f32[1,64,256]{2,1,0:T(8,128)S(1)} %get-tuple-element.43), channel_id=1, source_target_pairs={{0,1},{1,2},{2,3},{3,4},{4,5},{5,6},{6,7},{7,8},{8,9},{9,10},{10,1... | collective-permute-start | bytes 196616 | tf_op jit(solution)/shard_map/ppermute | solution.py:15
  117.2 116.5 %collective-permute-start.11 = (f32[1,64,256]{2,1,0:T(8,128)S(1)}, f32[1,64,256]{2,1,0:T(8,128)S(1)}, u32[]{:S(2)}, u32[]{:S(2)}) collective-permute-start(f32[1,64,256]{2,1,0:T(8,128)S(1)} %get-tuple-element.42), channel_id=1, source_target_pairs={{1,0},{2,1},{3,2},{4,3},{5,4},{6,5},{7,6},{8,7},{9,8},{10,9},{11,1... | collective-permute-start | bytes 196616 | tf_op jit(solution)/shard_map/ppermute | solution.py:18
  119.1 114.6 %collective-permute-start.10 = (f32[1,64,256]{2,1,0:T(8,128)S(1)}, f32[1,64,256]{2,1,0:T(8,128)S(1)}, u32[]{:S(2)}, u32[]{:S(2)}) collective-permute-start(f32[1,64,256]{2,1,0:T(8,128)S(1)} %get-tuple-element.41), channel_id=1, source_target_pairs={{0,1},{1,2},{2,3},{3,4},{4,5},{5,6},{6,7},{7,8},{8,9},{9,10},{10,1... | collective-permute-start | bytes 196616 | tf_op jit(solution)/shard_map/ppermute | solution.py:15
  122.5 161.6 %collective-permute-start.1 = (f32[1,32,128]{2,1,0:T(8,128)S(1)}, f32[1,32,128]{2,1,0:T(8,128)S(1)}, u32[]{:S(2)}, u32[]{:S(2)}) collective-permute-start(f32[1,32,128]{2,1,0:T(8,128)S(1)} %get-tuple-element.80), channel_id=1, source_target_pairs={{1,0},{2,1},{3,2},{4,3},{5,4},{6,5},{7,6},{8,7},{9,8},{10,9},{11,1... | collective-permute-start | bytes 49160 | tf_op jit(solution)/shard_map/ppermute | solution.py:18
  131.3 152.7 %collective-permute-start = (f32[1,32,128]{2,1,0:T(8,128)S(1)}, f32[1,32,128]{2,1,0:T(8,128)S(1)}, u32[]{:S(2)}, u32[]{:S(2)}) collective-permute-start(f32[1,32,128]{2,1,0:T(8,128)S(1)} %get-tuple-element.79), channel_id=1, source_target_pairs={{0,1},{1,2},{2,3},{3,4},{4,5},{5,6},{6,7},{7,8},{8,9},{9,10},{10,1... | collective-permute-start | bytes 49160 | tf_op jit(solution)/shard_map/ppermute | solution.py:15
  284.2 12.4 %collective-permute-start.3 = (f32[1,32,128]{2,1,0:T(8,128)S(1)}, f32[1,32,128]{2,1,0:T(8,128)S(1)}, u32[]{:S(2)}, u32[]{:S(2)}) collective-permute-start(f32[1,32,128]{2,1,0:T(8,128)S(1)} %get-tuple-element.78), channel_id=1, source_target_pairs={{1,0},{2,1},{3,2},{4,3},{5,4},{6,5},{7,6},{8,7},{9,8},{10,9},{11,1... | collective-permute-start | bytes 49160 | tf_op jit(solution)/shard_map/ppermute | solution.py:18
  294.5 11.4 %collective-permute-start.2 = (f32[1,32,128]{2,1,0:T(8,128)S(1)}, f32[1,32,128]{2,1,0:T(8,128)S(1)}, u32[]{:S(2)}, u32[]{:S(2)}) collective-permute-start(f32[1,32,128]{2,1,0:T(8,128)S(1)} %get-tuple-element.77), channel_id=1, source_target_pairs={{0,1},{1,2},{2,3},{3,4},{4,5},{5,6},{6,7},{7,8},{8,9},{9,10},{10,1... | collective-permute-start | bytes 49160 | tf_op jit(solution)/shard_map/ppermute | solution.py:15
  343.1 11.5 %collective-permute-start.13 = (f32[1,32,128]{2,1,0:T(8,128)S(1)}, f32[1,32,128]{2,1,0:T(8,128)S(1)}, u32[]{:S(2)}, u32[]{:S(2)}) collective-permute-start(f32[1,32,128]{2,1,0:T(8,128)S(1)} %get-tuple-element.75), channel_id=1, source_target_pairs={{0,1},{1,2},{2,3},{3,4},{4,5},{5,6},{6,7},{7,8},{8,9},{9,10},{10,1... | collective-permute-start | bytes 49160 | tf_op jit(solution)/shard_map/ppermute | solution.py:15
  356.6 11.4 %collective-permute-start.15 = (f32[1,32,128]{2,1,0:T(8,128)S(1)}, f32[1,32,128]{2,1,0:T(8,128)S(1)}, u32[]{:S(2)}, u32[]{:S(2)}) collective-permute-start(f32[1,32,128]{2,1,0:T(8,128)S(1)} %get-tuple-element.73), channel_id=1, source_target_pairs={{0,1},{1,2},{2,3},{3,4},{4,5},{5,6},{6,7},{7,8},{8,9},{9,10},{10,1... | collective-permute-start | bytes 49160 | tf_op jit(solution)/shard_map/ppermute | solution.py:15
  377.5 11.4 %collective-permute-start.18 = (f32[1,32,128]{2,1,0:T(8,128)S(1)}, f32[1,32,128]{2,1,0:T(8,128)S(1)}, u32[]{:S(2)}, u32[]{:S(2)}) collective-permute-start(f32[1,32,128]{2,1,0:T(8,128)S(1)} %get-tuple-element.71), channel_id=1, source_target_pairs={{0,1},{1,2},{2,3},{3,4},{4,5},{5,6},{6,7},{7,8},{8,9},{9,10},{10,1... | collective-permute-start | bytes 49160 | tf_op jit(solution)/shard_map/ppermute | solution.py:15
  390.9 11.4 %collective-permute-start.20 = (f32[1,32,128]{2,1,0:T(8,128)S(1)}, f32[1,32,128]{2,1,0:T(8,128)S(1)}, u32[]{:S(2)}, u32[]{:S(2)}) collective-permute-start(f32[1,32,128]{2,1,0:T(8,128)S(1)} %get-tuple-element.69), channel_id=1, source_target_pairs={{0,1},{1,2},{2,3},{3,4},{4,5},{5,6},{6,7},{7,8},{8,9},{9,10},{10,1... | collective-permute-start | bytes 49160 | tf_op jit(solution)/shard_map/ppermute | solution.py:15
  411.9 11.4 %collective-permute-start.23 = (f32[1,32,128]{2,1,0:T(8,128)S(1)}, f32[1,32,128]{2,1,0:T(8,128)S(1)}, u32[]{:S(2)}, u32[]{:S(2)}) collective-permute-start(f32[1,32,128]{2,1,0:T(8,128)S(1)} %get-tuple-element.67), channel_id=1, source_target_pairs={{0,1},{1,2},{2,3},{3,4},{4,5},{5,6},{6,7},{7,8},{8,9},{9,10},{10,1... | collective-permute-start | bytes 49160 | tf_op jit(solution)/shard_map/ppermute | solution.py:15
  425.4 11.4 %collective-permute-start.25 = (f32[1,32,128]{2,1,0:T(8,128)S(1)}, f32[1,32,128]{2,1,0:T(8,128)S(1)}, u32[]{:S(2)}, u32[]{:S(2)}) collective-permute-start(f32[1,32,128]{2,1,0:T(8,128)S(1)} %get-tuple-element.65), channel_id=1, source_target_pairs={{0,1},{1,2},{2,3},{3,4},{4,5},{5,6},{6,7},{7,8},{8,9},{9,10},{10,1... | collective-permute-start | bytes 49160 | tf_op jit(solution)/shard_map/ppermute | solution.py:15
  446.3 11.4 %collective-permute-start.28 = (f32[1,32,128]{2,1,0:T(8,128)S(1)}, f32[1,32,128]{2,1,0:T(8,128)S(1)}, u32[]{:S(2)}, u32[]{:S(2)}) collective-permute-start(f32[1,32,128]{2,1,0:T(8,128)S(1)} %get-tuple-element.63), channel_id=1, source_target_pairs={{0,1},{1,2},{2,3},{3,4},{4,5},{5,6},{6,7},{7,8},{8,9},{9,10},{10,1... | collective-permute-start | bytes 49160 | tf_op jit(solution)/shard_map/ppermute | solution.py:15
  459.8 11.4 %collective-permute-start.30 = (f32[1,32,128]{2,1,0:T(8,128)S(1)}, f32[1,32,128]{2,1,0:T(8,128)S(1)}, u32[]{:S(2)}, u32[]{:S(2)}) collective-permute-start(f32[1,32,128]{2,1,0:T(8,128)S(1)} %get-tuple-element.61), channel_id=1, source_target_pairs={{0,1},{1,2},{2,3},{3,4},{4,5},{5,6},{6,7},{7,8},{8,9},{9,10},{10,1... | collective-permute-start | bytes 49160 | tf_op jit(solution)/shard_map/ppermute | solution.py:15
  480.8 11.4 %collective-permute-start.33 = (f32[1,32,128]{2,1,0:T(8,128)S(1)}, f32[1,32,128]{2,1,0:T(8,128)S(1)}, u32[]{:S(2)}, u32[]{:S(2)}) collective-permute-start(f32[1,32,128]{2,1,0:T(8,128)S(1)} %get-tuple-element.59), channel_id=1, source_target_pairs={{0,1},{1,2},{2,3},{3,4},{4,5},{5,6},{6,7},{7,8},{8,9},{9,10},{10,1... | collective-permute-start | bytes 49160 | tf_op jit(solution)/shard_map/ppermute | solution.py:15
  494.2 11.4 %collective-permute-start.35 = (f32[1,32,128]{2,1,0:T(8,128)S(1)}, f32[1,32,128]{2,1,0:T(8,128)S(1)}, u32[]{:S(2)}, u32[]{:S(2)}) collective-permute-start(f32[1,32,128]{2,1,0:T(8,128)S(1)} %get-tuple-element.57), channel_id=1, source_target_pairs={{0,1},{1,2},{2,3},{3,4},{4,5},{5,6},{6,7},{7,8},{8,9},{9,10},{10,1... | collective-permute-start | bytes 49160 | tf_op jit(solution)/shard_map/ppermute | solution.py:15
  515.2 11.4 %collective-permute-start.38 = (f32[1,32,128]{2,1,0:T(8,128)S(1)}, f32[1,32,128]{2,1,0:T(8,128)S(1)}, u32[]{:S(2)}, u32[]{:S(2)}) collective-permute-start(f32[1,32,128]{2,1,0:T(8,128)S(1)} %get-tuple-element.55), channel_id=1, source_target_pairs={{0,1},{1,2},{2,3},{3,4},{4,5},{5,6},{6,7},{7,8},{8,9},{9,10},{10,1... | collective-permute-start | bytes 49160 | tf_op jit(solution)/shard_map/ppermute | solution.py:15
  528.6 11.4 %collective-permute-start.40 = (f32[1,32,128]{2,1,0:T(8,128)S(1)}, f32[1,32,128]{2,1,0:T(8,128)S(1)}, u32[]{:S(2)}, u32[]{:S(2)}) collective-permute-start(f32[1,32,128]{2,1,0:T(8,128)S(1)} %get-tuple-element.53), channel_id=1, source_target_pairs={{0,1},{1,2},{2,3},{3,4},{4,5},{5,6},{6,7},{7,8},{8,9},{9,10},{10,1... | collective-permute-start | bytes 49160 | tf_op jit(solution)/shard_map/ppermute | solution.py:15
  (23 other events, 151.1 us)
where the time goes:
time: 582 us; the launch traced here: 576 us
  starting transfers between devices  183 us (31%)
  local copies, waits for them, and re-layouts  156 us (27%)
  waiting for transfers between devices  141 us (24%)
  other arithmetic  95 us (16%)
    ppermute x20, waiting for transfers between devices, padded_2(): lax.ppermute(lax.slice_in_dim(block, block.shape[dim] - width, None, axis...  134 us
    reshape x7, local copies, waits for them, and re-layouts, coarsen(): field.reshape(first // 2, 2, second // 2, 2, third // 2, 2)  127 us
    ppermute x20, starting transfers between devices, padded_2(): lax.ppermute(lax.slice_in_dim(block, 0, width, axis=dim), axis, backward)  75.9 us
    ppermute x20, starting transfers between devices, padded_2(): lax.ppermute(lax.slice_in_dim(block, block.shape[dim] - width, None, axis...  60.2 us
    reduce_sum x8, other arithmetic, coarsen(): field.reshape(first // 2, 2, second // 2, 2, third // 2, 2)  55.8 us
    ppermute x7, starting transfers between devices, from_behind(): return lax.ppermute(block, axis, route)  47 us
    another operation x1, local copies, waits for them, and re-layouts, coarsen(): field.reshape(first // 2, 2, second // 2, 2, third // 2, 2)  18.8 us
    add x13, other arithmetic, advance(): return middle + time_step * change / retardation  18.7 us
  transfers between devices with their start and end apart: 47, of which 24 were waited for; matrix products, arithmetic and copies ran while one was open for 32% of the time, Pallas kernels for 0%

commit v1 on v0

v1 whole, which is shorter than its diff:
```python
import jax
import jax.numpy as jnp
from jax import lax
from jax.experimental import pallas as pl
from jax.experimental.pallas import tpu as pltpu
from jax.sharding import PartitionSpec as P

MESH = pl.DeviceIdType.MESH
F32 = jnp.float32
MATS = 12
TILES = 32
HALF = 128
FY = 64
CY = 32
PAD = 8
WIDE = 4


def lane(rows):
    return lax.broadcasted_iota(jnp.int32, (rows, HALF), 1)


def roll(value, shift):
    return pltpu.roll(value, shift, 1)


def gather(value, index):
    return jnp.take_along_axis(value, index, axis=1)


def update(um, u0, up, ym, yp, zm, zp, a, b, c, d, kn, n1):
    flux = a * ((up + zp) + (ym + yp)) + b * um + c * zm - d * u0
    power = jnp.exp2(n1 * jnp.log2(jnp.abs(u0) + 1.0))
    return u0 + flux / (1.0 + kn * power)


def squeeze_lanes(low, high):
    rows = low.shape[0]
    at = lane(rows)
    index = (2 * at) % HALF
    low = low + roll(low, HALF - 1)
    high = high + roll(high, HALF - 1)
    return jnp.where(at < HALF // 2, gather(low, index), gather(high, index))


def kernel(
    cond, disp, fk, fn, load, init, mat, out,
    U, M, C, L, LD, FL, GC, GU, GG, OWN, SEND, W, CF, CC, RD, GCB, FWB, OUT,
    in_sem, halo_send, halo_recv, cf_send, cf_recv, s_send, s_recv, fw_send, fw_recv,
):
    m = lax.axis_index("tm")
    t = lax.axis_index("tile")

    def device(tm, tile):
        return {"tm": tm, "tile": tile}

    def inside(tile):
        return jnp.logical_and(tile >= 0, tile < TILES)

    lead = jnp.logical_or(m == 3, m == 7)
    count = jnp.where(m == 3, 3, 4)
    first = jnp.where(m == 3, 0, 3)
    head = jnp.where(m < 3, 3, 7)
    place = jnp.where(m < 3, m, m - 3)
    width = head - m
    reach = jnp.where(m == 7, 4, jnp.where(m == 3, 3, 1))
    has = (t < TILES - 1, t > 0)

    loads = []
    for h in range(2):
        loads.append(pltpu.make_async_copy(mat.at[:, :, pl.ds(HALF * h, HALF)], M.at[pl.ds(2, 4), h], in_sem.at[h]))
    for h in range(2):
        loads.append(
            pltpu.make_async_copy(
                init.at[0, :, :, pl.ds(HALF * h, HALF)], U.at[0, pl.ds(3, 4), h, pl.ds(PAD, FY), :], in_sem.at[2 + h]
            )
        )
    for copy in loads:
        copy.start()

    zero = jnp.zeros((PAD, HALF), F32)

    def blank_fine(i, carry):
        for h in range(2):
            U[i // 10, i % 10, h, pl.ds(0, PAD), :] = zero
            U[i // 10, i % 10, h, pl.ds(PAD + FY, PAD), :] = zero
        return carry

    lax.fori_loop(0, 50, blank_fine, 0)

    def blank_coarse(i, carry):
        for k in range(2):
            W[k, i, pl.ds(0, PAD), :] = zero
            W[k, i, pl.ds(PAD + CY, PAD), :] = zero
        return carry

    lax.fori_loop(0, 18, blank_coarse, 0)
    for k in range(2):
        for r in range(6):
            GU[k, r, pl.ds(0, PAD), :] = zero
            GU[k, r, pl.ds(PAD + CY, PAD), :] = zero
    for s in range(2):

        @pl.when(jnp.logical_not(has[s]))
        def _():
            def clear(i, carry):
                for h in range(2):
                    U[i // 3, 7 - 7 * s + i % 3, h, pl.ds(PAD, FY), :] = jnp.zeros((FY, HALF), F32)
                return carry

            lax.fori_loop(0, 12, clear, 0)
            for k in range(2):
                for r in range(2):
                    GU[k, 4 - 4 * s + r, pl.ds(PAD, CY), :] = jnp.zeros((CY, HALF), F32)

    @pl.when(lead)
    def _():
        def clear(i, carry):
            @pl.when(jnp.logical_not(inside(t + i // 2 - WIDE)))
            def _():
                for f in range(5):
                    CF[i, f] = jnp.zeros((CY, HALF), F32)
                for j in range(4):
                    RD[j, i] = jnp.zeros((CY, HALF), F32)

            return carry

        lax.fori_loop(0, 18, clear, 0)

    barrier = pltpu.get_barrier_semaphore()

    def greet(tm, tile, when):
        @pl.when(jnp.logical_and(when, inside(tile)))
        def _():
            pl.semaphore_signal(barrier, inc=1, device_id=device(tm, tile), device_id_type=MESH)

    def greet_all(i, carry):
        d = i - WIDE
        greet(m, t + d, jnp.logical_and(d != 0, jnp.abs(d) <= reach))
        for j in range(4):
            greet(first + j, t + d, jnp.logical_and(jnp.logical_and(lead, j < count), jnp.abs(d) <= count - j))
        return carry

    lax.fori_loop(0, 2 * WIDE + 1, greet_all, 0)
    greet(head, t, jnp.logical_and(jnp.logical_not(lead), m > 0))

    def span(reach):
        return jnp.minimum(t, reach) + jnp.minimum(TILES - 1 - t, reach)

    expected = span(reach) + jnp.where(m == 7, 0, span(width) + 1) + jnp.where(lead, count - 1, 0)

    at = lane(8)
    tables = []
    for ref in (cond, disp, fk, fn):
        table = jnp.zeros((8, HALF), F32)
        for i in range(MATS):
            table = jnp.where(at == i, ref[i], table)
        tables.append(table)
    t_cond, t_disp, t_k, t_n = tables
    t_a = t_disp * t_cond
    tables = [t_a, t_a + 0.5 * t_cond, t_a + 0.3 * t_cond, 6.0 * t_a + 0.8 * t_cond, t_k * t_n, t_n - 1.0, t_k]

    def look_up(r):
        for h in range(2):
            index = M[r, h]
            for f, table in enumerate(tables):
                value = gather(jnp.broadcast_to(table[0:1], (FY, HALF)), index)
                if f == 2 and h == 0:
                    value = jnp.where(lane(FY) == 0, 1.0, value)
                C[f, r, h] = value

    def spread_load(s, i, r):
        row = jnp.broadcast_to(L[s, i : i + 1, :], (FY, HALF))
        here = lax.broadcasted_iota(jnp.int32, (FY, HALF), 0) == lane(FY)
        total = jnp.sum(jnp.where(here, row, 0.0), axis=1, keepdims=True)
        LD[r] = jnp.broadcast_to(total, (FY, HALF))

    def coarse_load(s, i):
        row = jnp.broadcast_to(L[s, i : i + 1, :] + L[s, i + 1 : i + 2, :], (CY, HALF))
        here = lax.broadcasted_iota(jnp.int32, (CY, HALF), 0) == lane(CY) // 2
        total = jnp.sum(jnp.where(here, row, 0.0), axis=1, keepdims=True)
        return jnp.broadcast_to(0.25 * total, (CY, HALF))

    def fine_step(k, r):
        for y in (0, 32):
            rows = pl.ds(PAD + y, 32)
            here = pl.ds(y, 32)
            low, high = U[k, r, 0, rows, :], U[k, r, 1, rows, :]
            at = lane(32)
            back = (roll(low, 1), roll(high, 1))
            ahead = (roll(low, HALF - 1), roll(high, HALF - 1))
            zms = (jnp.where(at == 0, LD[r - 1, here], back[0]), jnp.where(at == 0, back[0], back[1]))
            zps = (jnp.where(at == HALF - 1, ahead[1], ahead[0]), jnp.where(at == HALF - 1, 0.0, ahead[1]))
            for h in range(2):
                U[k + 1, r, h, rows, :] = update(
                    U[k, r - 1, h, rows, :],
                    (low, high)[h],
                    U[k, r + 1, h, rows, :],
                    U[k, r, h, pl.ds(PAD + y - 1, 32), :],
                    U[k, r, h, pl.ds(PAD + y + 1, 32), :],
                    zms[h],
                    zps[h],
                    *[C[f, r - 1, h, here] for f in range(6)],
                )

    def mean_rows(k, r):
        halves = []
        for h in range(2):
            parts = [U[k, r + q, h, pl.ds(PAD + p, CY, stride=2), :] for q in range(2) for p in range(2)]
            halves.append((parts[0] + parts[1]) + (parts[2] + parts[3]))
        return 0.125 * squeeze_lanes(*halves)

    def mean_coefs(j):
        means = []
        for f in (0, 1, 6, 5):
            halves = []
            for h in range(2):
                parts = [C[f, 2 * j + q, h, pl.ds(p, CY, stride=2), :] for q in range(2) for p in range(2)]
                halves.append((parts[0] + parts[1]) + (parts[2] + parts[3]))
            means.append(0.125 * squeeze_lanes(*halves))
        FL[j, 0] = 0.5 * means[0]
        FL[j, 1] = 2.0 * (means[1] - means[0])
        FL[j, 2] = means[2] * (means[3] + 1.0)
        FL[j, 3] = means[3]

    def combine(src, dst, r):
        a, cond = src[r, 0], src[r, 1]
        dst[r, 0] = a
        dst[r, 1] = a + 0.5 * cond
        dst[r, 2] = jnp.where(lane(CY) == 0, 1.0, a + 0.3 * cond)
        dst[r, 3] = 6.0 * a + 0.8 * cond
        dst[r, 4] = src[r, 2]
        dst[r, 5] = src[r, 3]

    def coarse_step(src, k, r, coefs, fields, place):
        rows = pl.ds(PAD, CY)
        at = lane(CY)
        u0 = src[k, r, rows, :]
        return update(
            src[k, r - 1, rows, :],
            u0,
            src[k, r + 1, rows, :],
            src[k, r, pl.ds(PAD - 1, CY), :],
            src[k, r, pl.ds(PAD + 1, CY), :],
            jnp.where(at == 0, fields[place, 4], roll(u0, 1)),
            jnp.where(at == HALF - 1, 0.0, roll(u0, HALF - 1)),
            *[coefs[place, f] for f in range(6)],
        )

    L[1] = jnp.zeros((8, HALF), F32)
    L[1, 0:4, 0:FY] = load[...]
    for i in range(4):
        spread_load(1, i, 2 + i)
    loads[0].wait()
    loads[1].wait()

    def own_rows(r, carry):
        look_up(r)
        return carry

    lax.fori_loop(2, 6, own_rows, 0)
    loads[2].wait()
    loads[3].wait()

    def inner_rows(r, carry):
        fine_step(0, r)
        return carry

    lax.fori_loop(4, 6, inner_rows, 0)
    for j in range(2):
        GU[0, 2 + j, pl.ds(PAD, CY), :] = mean_rows(0, 3 + 2 * j)

    pl.semaphore_wait(barrier, expected)

    rows = pl.ds(PAD, FY)

    def halo(item, s, arriving):
        src, dst = (
            (U.at[0, 3 + 3 * s, :, rows, :], U.at[0, 7 - 5 * s, :, rows, :]),
            (L.at[1], L.at[2 - 2 * s]),
            (M.at[pl.ds(2 + 2 * s, 2)], M.at[pl.ds(6 - 6 * s, 2)]),
            (U.at[0, 4 + s, :, rows, :], U.at[0, 8 - 7 * s, :, rows, :]),
            (GU.at[0, 3 - s, pl.ds(PAD, CY), :], GU.at[0, 5 - 5 * s, pl.ds(PAD, CY), :]),
            (U.at[1, pl.ds(4, 2), :, rows, :], U.at[1, pl.ds(8 - 8 * s, 2), :, rows, :]),
        )[item]
        toward = 2 * s - 1
        return pltpu.make_async_remote_copy(
            src_ref=src,
            dst_ref=dst,
            send_sem=halo_send.at[item, s],
            recv_sem=halo_recv.at[item, s],
            device_id=device(m, t - toward if arriving else t + toward),
            device_id_type=MESH,
        )

    sends = (t > 0, t < TILES - 1)
    for item in range(6):
        for s in range(2):

            @pl.when(sends[s])
            def _():
                halo(item, s, False).start()

    def arrive(items):
        for item in items:
            for s in range(2):

                @pl.when(has[s])
                def _():
                    halo(item, s, True).wait_recv()

    def both_sides(k, near):
        for s in range(2):
            r = 3 + (near if s == 1 else 3 - near)
            if near >= 0:
                fine_step(k, r)
            else:

                @pl.when(has[s])
                def _():
                    fine_step(k, r)

    for j in range(2):
        FL[1 + j, 4] = coarse_load(1, 2 * j)
        mean_coefs(1 + j)

    def coefs_copy(d, arriving):
        return pltpu.make_async_remote_copy(
            src_ref=FL.at[pl.ds(1, 2)],
            dst_ref=CF.at[pl.ds(2 * (WIDE + d if arriving else WIDE - d), 2)],
            send_sem=cf_send.at[WIDE + d],
            recv_sem=cf_recv.at[WIDE + d if arriving else WIDE - d],
            device_id=device(m, t + d),
            device_id_type=MESH,
        )

    def over_window(reach, act):
        def body(i, carry):
            d = i - WIDE

            @pl.when(jnp.logical_and(jnp.abs(d) <= reach, inside(t + d)))
            def _():
                act(d)

            return carry

        lax.fori_loop(0, 2 * WIDE + 1, body, 0)

    @pl.when(lead)
    def _():
        for q in range(2):
            CF[2 * WIDE + q] = FL[1 + q]

        def send(d):
            @pl.when(d != 0)
            def _():
                coefs_copy(d, False).start()

        over_window(reach, send)

    arrive((0,))
    both_sides(0, 0)
    both_sides(1, 1)
    arrive((1, 2, 3))
    for s in range(2):

        @pl.when(has[s])
        def _():
            for q in range(2):
                r = 6 - 6 * s + q
                look_up(r)
                spread_load(2 - 2 * s, q + 2 * s, r)
            FL[3 - 3 * s, 4] = coarse_load(2 - 2 * s, 2 * s)
            mean_coefs(3 - 3 * s)
            GU[0, 4 - 3 * s, pl.ds(PAD, CY), :] = mean_rows(0, 7 - 6 * s)

    both_sides(0, -1)
    both_sides(1, 0)
    both_sides(2, 1)

    arrive((4,))
    for j in (1, 2):
        combine(FL, GC, j)
        GU[1, 1 + j, pl.ds(PAD, CY), :] = coarse_step(GU, 0, 1 + j, GC, FL, j)
    for s in range(2):

        @pl.when(has[s])
        def _():
            j = 3 - 3 * s
            combine(FL, GC, j)
            GU[1, 1 + j, pl.ds(PAD, CY), :] = coarse_step(GU, 0, 1 + j, GC, FL, j)

    for j in (1, 2):
        GG[j - 1] = coarse_step(GU, 1, 1 + j, GC, FL, j)

    arrive((5,))
    both_sides(1, -2)
    both_sides(1, -1)
    both_sides(2, -1)
    both_sides(2, 0)
    both_sides(3, 0)
    both_sides(3, 1)

    for j in range(2):
        mean = mean_rows(4, 3 + 2 * j)
        OWN[j] = jnp.where(m == 0, mean, mean - GG[j])

    def block_copy(src, tm, tile, j, slot, at):
        return pltpu.make_async_remote_copy(
            src_ref=src,
            dst_ref=RD.at[j, pl.ds(2 * slot, 2)],
            send_sem=s_send.at[at],
            recv_sem=s_recv.at[j, slot],
            device_id=device(tm, tile),
            device_id_type=MESH,
        )

    def send_block(src):
        over_window(width, lambda d: block_copy(src, head, t + d, place, WIDE - d, WIDE + d).start())

    def sent_block(src):
        over_window(width, lambda d: block_copy(src, head, t + d, place, WIDE - d, WIDE + d).wait_send())

    @pl.when(jnp.logical_not(lead))
    def _():
        send_block(OWN)

    def forward(j, tm):
        return pltpu.make_async_remote_copy(
            src_ref=GCB.at[j],
            dst_ref=FWB,
            send_sem=fw_send.at[j],
            recv_sem=fw_recv.at[0],
            device_id=device(tm, t),
            device_id_type=MESH,
        )

    @pl.when(lead)
    def _():
        over_window(reach, lambda d: pl.when(d != 0)(lambda: coefs_copy(d, True).wait_recv()))

        def prepare(r, carry):
            combine(CF, CC, r)
            return carry

        lax.fori_loop(2 * (WIDE - count), 2 * (WIDE + count + 1), prepare, 0)

        def chain(j, carry):
            def take(d):
                block_copy(OWN, first + j, t + d, j, WIDE + d, WIDE + d).wait_recv()

            over_window(count - j, take)
            w = count - 1 - j

            @pl.when(j == 0)
            def _():
                def lay(r, carry):
                    W[0, r, pl.ds(PAD, CY), :] = RD[0, r]
                    return carry

                lax.fori_loop(2 * (WIDE - count), 2 * (WIDE + count + 1), lay, 0)

            @pl.when(j > 0)
            def _():
                def add(r, carry):
                    W[0, r, pl.ds(PAD, CY), :] = W[0, r, pl.ds(PAD, CY), :] + RD[j, r]
                    return carry

                lax.fori_loop(2 * (WIDE - w - 1), 2 * (WIDE + w + 2), add, 0)

            def one(i, carry):
                for q in range(2):
                    r = 2 * (WIDE - w) - 1 + 2 * i + q
                    W[1, r, pl.ds(PAD, CY), :] = coarse_step(W, 0, r, CC, CF, r)
                return carry

            lax.fori_loop(0, 2 * w + 2, one, 0)

            def two(i, carry):
                for q in range(2):
                    r = 2 * (WIDE - w) + 2 * i + q
                    W[0, r, pl.ds(PAD, CY), :] = coarse_step(W, 1, r, CC, CF, r)
                return carry

            lax.fori_loop(0, 2 * w + 1, two, 0)
            for q in range(2):
                GCB[j, q] = W[0, 2 * WIDE + q, pl.ds(PAD, CY), :]
            return carry

        lax.fori_loop(0, count, chain, 0)

        @pl.when(m == 3)
        def _():
            for q in range(2):
                SEND[q] = GCB[2, q] + OWN[q]
            send_block(SEND)

        def hand_on(j, carry):
            forward(j, first + 1 + j).start()
            return carry

        lax.fori_loop(0, count - 1, hand_on, 0)
        for q in range(2):
            FWB[q] = GCB[count - 1, q]

    @pl.when(m == 0)
    def _():
        for q in range(2):
            FWB[q] = GG[q]

    @pl.when(jnp.logical_not(jnp.logical_or(lead, m == 0)))
    def _():
        forward(0, head).wait_recv()

    for j in range(2):
        shift = FWB[j] - GG[j]
        for h in range(2):
            wide = gather(shift, lane(CY) // 2 + 64 * h)
            for q in range(2):
                for p in range(2):
                    OUT[2 * j + q, h, pl.ds(p, CY, stride=2), :] = (
                        U[4, 3 + 2 * j + q, h, pl.ds(PAD + p, CY, stride=2), :] + wide
                    )
    stores = [
        pltpu.make_async_copy(OUT.at[:, h], out.at[0, :, :, pl.ds(HALF * h, HALF)], in_sem.at[h]) for h in range(2)
    ]
    for copy in stores:
        copy.start()

    for item in range(6):
        for s in range(2):

            @pl.when(sends[s])
            def _():
                halo(item, s, False).wait_send()

    @pl.when(lead)
    def _():
        over_window(reach, lambda d: pl.when(d != 0)(lambda: coefs_copy(d, False).wait_send()))

        def handed(j, carry):
            forward(j, first + 1 + j).wait_send()
            return carry

        lax.fori_loop(0, count - 1, handed, 0)

    @pl.when(jnp.logical_not(lead))
    def _():
        sent_block(OWN)

    @pl.when(m == 3)
    def _():
        sent_block(SEND)

    for copy in stores:
        copy.wait()


def shards(initial_states, material, conductivity, dispersivity, freundlich_k, freundlich_n, surface_load):
    smem = pl.BlockSpec(memory_space=pltpu.SMEM)
    anywhere = pl.BlockSpec(memory_space=pl.ANY)
    vmem = pl.BlockSpec(memory_space=pltpu.VMEM)
    block = (CY, HALF)
    dma = pltpu.SemaphoreType.DMA
    return pl.pallas_call(
        kernel,
        out_shape=jax.ShapeDtypeStruct(initial_states.shape, F32),
        in_specs=[smem] * 4 + [vmem, anywhere, anywhere],
        out_specs=anywhere,
        scratch_shapes=[
            pltpu.VMEM((5, 10, 2, FY + 2 * PAD, HALF), F32),
            pltpu.VMEM((8, 2, FY, HALF), jnp.int32),
            pltpu.VMEM((7, 8, 2, FY, HALF), F32),
            pltpu.VMEM((3, 8, HALF), F32),
            pltpu.VMEM((8, FY, HALF), F32),
            pltpu.VMEM((4, 5) + block, F32),
            pltpu.VMEM((4, 6) + block, F32),
            pltpu.VMEM((2, 6, CY + 2 * PAD, HALF), F32),
            pltpu.VMEM((2,) + block, F32),
            pltpu.VMEM((2,) + block, F32),
            pltpu.VMEM((2,) + block, F32),
            pltpu.VMEM((2, 4 * WIDE + 2, CY + 2 * PAD, HALF), F32),
            pltpu.VMEM((4 * WIDE + 2, 5) + block, F32),
            pltpu.VMEM((4 * WIDE + 2, 6) + block, F32),
            pltpu.VMEM((4, 4 * WIDE + 2) + block, F32),
            pltpu.VMEM((4, 2) + block, F32),
            pltpu.VMEM((2,) + block, F32),
            pltpu.VMEM((4, 2, FY, HALF), F32),
            dma((4,)),
            dma((6, 2)),
            dma((6, 2)),
            dma((2 * WIDE + 1,)),
            dma((2 * WIDE + 1,)),
            dma((2 * WIDE + 1,)),
            dma((4, 2 * WIDE + 1)),
            dma((4,)),
            dma((1,)),
        ],
        compiler_params=pltpu.CompilerParams(
            collective_id=0, has_side_effects=True, vmem_limit_bytes=40 * 1024 * 1024
        ),
    )(conductivity, dispersivity, freundlich_k, freundlich_n, surface_load, initial_states, material)


def solution(mesh):
    in_specs = (
        P("tm", "tile", None, None),
        P("tile", None, None),
        P(),
        P(),
        P(),
        P(),
        P("tile", None),
    )
    out_specs = P("tm", "tile", None, None)
    return jax.shard_map(shards, mesh=mesh, in_specs=in_specs, out_specs=out_specs, check_vma=False)
```

time: 582 us -> 73.7 us (0.13); the launches traced: 576 us -> 73.5 us
  starting transfers between devices: 183 us -> 0 us
  local copies, waits for them, and re-layouts: 156 us -> 5.9 us
  waiting for transfers between devices: 141 us -> 0 us
  other arithmetic: 95 us -> 0 us
  Pallas kernels: 0 us -> 67.6 us
    ppermute x47 -> x0, starting transfers between devices: 183 us -> none  [the longest x20 75.9 us: padded_2(): lax.ppermute(lax.slice_in_dim(block, 0, width, axis=dim), axis, backward)]
    ppermute x47 -> x0, waiting for transfers between devices: 141 us -> none  [the longest x20 134 us: padded_2(): lax.ppermute(lax.slice_in_dim(block, block.shape[dim] - width, None, axis...]
    reshape x11 -> x0, local copies, waits for them, and re-layouts: 127 us -> none  [the longest x7 127 us: coarsen(): field.reshape(first // 2, 2, second // 2, 2, third // 2, 2)]
    pallas_call x0 -> x1, Pallas kernels: none -> 67.6 us  [shards(): pl.pallas_call(kernel, out_shape=jax.ShapeDtypeStruct(initial_states.shap...]
    reduce_sum x8 -> x0, other arithmetic: 55.8 us -> none  [coarsen(): field.reshape(first // 2, 2, second // 2, 2, third // 2, 2)]
    add x20 -> x0, other arithmetic: 19.3 us -> none  [the longest x13 18.7 us: advance(): return middle + time_step * change / retardation]
    sub x5 -> x0, other arithmetic: 19 us -> none  [the longest x4 18.6 us: advance(): spread / (spacing * spacing) * (neighbours - 6.0 * middle)]
    another operation x1 -> x0, local copies, waits for them, and re-layouts: 18.8 us -> none  [coarsen(): field.reshape(first // 2, 2, second // 2, 2, third // 2, 2)]
  transfers between devices with their start and end apart: 47 -> 0, of which waited for: 24 -> 0; matrix products, arithmetic and copies ran while one was open for 32% -> 0% of each run, Pallas kernels for 0% -> 0%
where the time goes in v1:
time: 73.7 us; the launch traced here: 73.5 us
  Pallas kernels  67.6 us (92%)
  local copies, waits for them, and re-layouts  5.9 us (8%)
    pallas_call x1, Pallas kernels, shards(): pl.pallas_call(kernel, out_shape=jax.ShapeDtypeStruct(initial_states.shap...  67.6 us
    unnamed x15, local copies, waits for them, and re-layouts  5.9 us

profile of v1, /device:TPU:89, one launch (start us, length us, event | category | flops | bytes accessed | tf_op | source)
XLA Modules:
  0.0 73.5 jit_solution(18397369466726787593)
XLA Ops:
  0.0 0.0 copy-start
  0.0 0.9 %copy-done = f32[1,4,64,256]{3,2,1,0:T(8,128)S(1)} copy-done((f32[1,4,64,256]{3,2,1,0:T(8,128)S(1)}, f32[1,4,64,256]{3,2,1,0:T(8,128)}, u32[]{:S(2)}) %copy-start) | copy-done | bytes 262168
  1.0 0.0 copy-start.1
  1.0 0.9 %copy-done.1 = s32[4,64,256]{2,1,0:T(8,128)S(1)} copy-done((s32[4,64,256]{2,1,0:T(8,128)S(1)}, s32[4,64,256]{2,1,0:T(8,128)}, u32[]{:S(2)}) %copy-start.1) | copy-done | bytes 262168
  1.9 0.0 copy-start.2
  1.9 0.7 copy-done.2
  2.6 0.0 copy-start.3
  2.6 0.7 copy-done.3
  3.2 0.0 copy-start.4
  3.2 0.7 copy-done.4
  3.9 0.0 copy-start.5
  3.9 0.7 copy-done.5
  4.6 0.0 copy-start.6
  4.6 0.7 copy-done.6
  5.2 67.6 %shard_map.73 = f32[1,4,64,256]{3,2,1,0:T(8,128)S(1)} custom-call(f32[12]{0:T(128)S(1)} %copy-done.3, f32[12]{0:T(128)S(1)} %copy-done.4, f32[12]{0:T(128)S(1)} %copy-done.5, f32[12]{0:T(128)S(1)} %copy-done.6, f32[4,64]{1,0:T(4,128)S(1)} %copy-done.2, f32[1,4,64,256]{3,2,1,0:T(8,128)S(1)} %copy-done, s32[4,64,256]{2,1,0:T(8,128)S(1)} %copy-done.1), custom_call_target="tpu_custom_call" | custom-call | tf_op jit(solution)/shard_map/pallas_call | solution.py:565
  72.8 0.7 copy.9
Async XLA Ops:
  0.0 0.9 %copy-start = (f32[1,4,64,256]{3,2,1,0:T(8,128)S(1)}, f32[1,4,64,256]{3,2,1,0:T(8,128)}, u32[]{:S(2)}) copy-start(f32[1,4,64,256]{3,2,1,0:T(8,128)} %init.1) | copy-start | bytes 786436
  1.0 0.9 %copy-start.1 = (s32[4,64,256]{2,1,0:T(8,128)S(1)}, s32[4,64,256]{2,1,0:T(8,128)}, u32[]{:S(2)}) copy-start(s32[4,64,256]{2,1,0:T(8,128)} %mat.1) | copy-start | bytes 786436
  1.9 0.7 copy-start.2
  2.6 0.7 copy-start.3
  3.2 0.7 copy-start.4
  3.9 0.7 copy-start.5
  4.6 0.7 copy-start.6

commit v2 on v1

--- a/solution.py
+++ b/solution.py
@@ -46,7 +46,7 @@
 def kernel(
     cond, disp, fk, fn, load, init, mat, out,
     U, M, C, L, LD, FL, GC, GU, GG, OWN, SEND, W, CF, CC, RD, GCB, FWB, OUT,
-    in_sem, halo_send, halo_recv, cf_send, cf_recv, s_send, s_recv, fw_send, fw_recv,
+    LIN, TAB, RU, in_sem, small_sem, halo_send, halo_recv, relay_send, relay_recv, sib_send, sib_recv, cf_send, cf_recv, s_send, s_recv, fw_send, fw_recv,
 ):
     m = lax.axis_index("tm")
     t = lax.axis_index("tile")
@@ -63,7 +63,24 @@
     head = jnp.where(m < 3, 3, 7)
     place = jnp.where(m < 3, m, m - 3)
     width = head - m
-    reach = jnp.where(m == 7, 4, jnp.where(m == 3, 3, 1))
+
+    def coefs_from(e, d):
+        far = jnp.abs(d)
+        return jnp.where(
+            e == 7,
+            jnp.where(far == 1, 5, jnp.where(far == 2, 2, jnp.where(far == 3, 0, 1))),
+            jnp.where(far == 1, 6, jnp.where(far == 2, 4, 5)),
+        )
+
+    def gives_coefs(e, d):
+        far = jnp.abs(d)
+        return jnp.logical_and(jnp.logical_and(far >= 1, far <= (4 if e == 7 else 3)), m == coefs_from(e, d))
+
+    x = t % 4
+    core = m % 2
+    sibling = m + 1 - 2 * core
+    far = (x == 0, x == 3)
+    relays = (jnp.logical_and(x == 2, t + 2 < TILES), jnp.logical_and(x == 1, t >= 2))
     has = (t < TILES - 1, t > 0)
 
     loads = []
@@ -75,8 +92,46 @@
                 init.at[0, :, :, pl.ds(HALF * h, HALF)], U.at[0, pl.ds(3, 4), h, pl.ds(PAD, FY), :], in_sem.at[2 + h]
             )
         )
-    for copy in loads:
+    small = [pltpu.make_async_copy(load, LIN, small_sem.at[0])]
+    for i, ref in enumerate((cond, disp, fk, fn)):
+        small.append(pltpu.make_async_copy(ref, TAB.at[i], small_sem.at[1 + i]))
+    for copy in loads + small:
         copy.start()
+
+    barrier = pltpu.get_barrier_semaphore()
+
+    def greet(tm, tile, when):
+        @pl.when(jnp.logical_and(when, inside(tile)))
+        def _():
+            pl.semaphore_signal(barrier, inc=1, device_id=device(tm, tile), device_id_type=MESH)
+
+    def greet_all(i, carry):
+        d = i - WIDE
+        greet(m, t + d, jnp.abs(d) == 1)
+        greet(coefs_from(m, d), t + d, jnp.logical_and(lead, jnp.logical_and(d != 0, jnp.abs(d) <= count)))
+        for j in range(4):
+            greet(first + j, t + d, jnp.logical_and(jnp.logical_and(lead, j < count), jnp.abs(d) <= count - j))
+        return carry
+
+    lax.fori_loop(0, 2 * WIDE + 1, greet_all, 0)
+    greet(head, t, jnp.logical_and(jnp.logical_not(lead), m > 0))
+
+    def span(reach):
+        return jnp.minimum(t, reach) + jnp.minimum(TILES - 1 - t, reach)
+
+    greet(sibling, t, m >= 0)
+
+    def add_coefs(i, total):
+        d = i - WIDE
+        for e in (3, 7):
+            total = total + jnp.where(jnp.logical_and(gives_coefs(e, d), inside(t + d)), 1, 0)
+        return total
+
+    expected = 1 + span(1) + jnp.where(m == 7, 0, span(width) + 1) + jnp.where(lead, count - 1, 0)
+    for s in range(2):
+        greet(m, t + 2 - 4 * s, relays[s])
+        expected = expected + jnp.where(jnp.logical_and(far[s], (t > 0, t < TILES - 1)[s]), 1, 0)
+    expected = expected + lax.fori_loop(0, 2 * WIDE + 1, add_coefs, 0)
 
     zero = jnp.zeros((PAD, HALF), F32)
 
@@ -127,34 +182,14 @@
 
         lax.fori_loop(0, 18, clear, 0)
 
-    barrier = pltpu.get_barrier_semaphore()
-
-    def greet(tm, tile, when):
-        @pl.when(jnp.logical_and(when, inside(tile)))
-        def _():
-            pl.semaphore_signal(barrier, inc=1, device_id=device(tm, tile), device_id_type=MESH)
-
-    def greet_all(i, carry):
-        d = i - WIDE
-        greet(m, t + d, jnp.logical_and(d != 0, jnp.abs(d) <= reach))
-        for j in range(4):
-            greet(first + j, t + d, jnp.logical_and(jnp.logical_and(lead, j < count), jnp.abs(d) <= count - j))
-        return carry
-
-    lax.fori_loop(0, 2 * WIDE + 1, greet_all, 0)
-    greet(head, t, jnp.logical_and(jnp.logical_not(lead), m > 0))
-
-    def span(reach):
-        return jnp.minimum(t, reach) + jnp.minimum(TILES - 1 - t, reach)
-
-    expected = span(reach) + jnp.where(m == 7, 0, span(width) + 1) + jnp.where(lead, count - 1, 0)
-
     at = lane(8)
     tables = []
-    for ref in (cond, disp, fk, fn):
+    for copy in small:
+        copy.wait()
+    for k in range(4):
         table = jnp.zeros((8, HALF), F32)
         for i in range(MATS):
-            table = jnp.where(at == i, ref[i], table)
+            table = jnp.where(at == i, TAB[k, i], table)
         tables.append(table)
     t_cond, t_disp, t_k, t_n = tables
     t_a = t_disp * t_cond
@@ -248,7 +283,7 @@
         )
 
     L[1] = jnp.zeros((8, HALF), F32)
-    L[1, 0:4, 0:FY] = load[...]
+    L[1, 0:4, 0:FY] = LIN[...]
     for i in range(4):
         spread_load(1, i, 2 + i)
     loads[0].wait()
@@ -277,11 +312,12 @@
     def halo(item, s, arriving):
         src, dst = (
             (U.at[0, 3 + 3 * s, :, rows, :], U.at[0, 7 - 5 * s, :, rows, :]),
+            (M.at[2 + 3 * s + core * (1 - 2 * s)], M.at[6 - 5 * s + core * (1 - 2 * s)]),
             (L.at[1], L.at[2 - 2 * s]),
-            (M.at[pl.ds(2 + 2 * s, 2)], M.at[pl.ds(6 - 6 * s, 2)]),
             (U.at[0, 4 + s, :, rows, :], U.at[0, 8 - 7 * s, :, rows, :]),
             (GU.at[0, 3 - s, pl.ds(PAD, CY), :], GU.at[0, 5 - 5 * s, pl.ds(PAD, CY), :]),
-            (U.at[1, pl.ds(4, 2), :, rows, :], U.at[1, pl.ds(8 - 8 * s, 2), :, rows, :]),
+            (U.at[1, 4, :, rows, :], U.at[1, 8 - 8 * s, :, rows, :]),
+            (U.at[1, 5, :, rows, :], U.at[1, 9 - 8 * s, :, rows, :]),
         )[item]
         toward = 2 * s - 1
         return pltpu.make_async_remote_copy(
@@ -293,13 +329,58 @@
             device_id_type=MESH,
         )
 
+    def by_relay(item, s, step):
+        toward = 2 * s - 1
+        q = item - 5
+        if step < 2:
+            return pltpu.make_async_remote_copy(
+                src_ref=U.at[1, 4 + q, :, rows, :],
+                dst_ref=RU.at[q],
+                send_sem=halo_send.at[item, s],
+                recv_sem=relay_recv.at[q],
+                device_id=device(m, t + 2 * toward if step == 0 else t - 2 * toward),
+                device_id_type=MESH,
+            )
+        return pltpu.make_async_remote_copy(
+            src_ref=RU.at[q],
+            dst_ref=U.at[1, 8 - 8 * s + q, :, rows, :],
+            send_sem=relay_send.at[q],
+            recv_sem=halo_recv.at[item, s],
+            device_id=device(m, t - toward),
+            device_id_type=MESH,
+        )
+
+    def to_sibling(s, arriving):
+        place = 6 - 5 * s + (1 - core if arriving else core) * (1 - 2 * s)
+        return pltpu.make_async_remote_copy(
+            src_ref=M.at[place],
+            dst_ref=M.at[place],
+            send_sem=sib_send.at[s],
+            recv_sem=sib_recv.at[s],
+            device_id=device(sibling, t),
+            device_id_type=MESH,
+        )
+
     sends = (t > 0, t < TILES - 1)
-    for item in range(6):
+
+    def each_send(act):
         for s in range(2):
 
-            @pl.when(sends[s])
+            @pl.when(jnp.logical_and(sends[s], far[s]))
             def _():
-                halo(item, s, False).start()
+                for item in (5, 6):
+                    act(by_relay(item, s, 0))
+                for item in (1, 2, 4, 0, 3):
+                    act(halo(item, s, False))
+
+        for item in (1, 2, 4, 0, 3, 5, 6):
+            for s in range(2):
+
+                @pl.when(jnp.logical_and(sends[s], jnp.logical_not(far[s])))
+                def _():
+                    act(halo(item, s, False))
+
+    each_send(lambda copy: copy.start())
 
     def arrive(items):
         for item in items:
@@ -324,13 +405,13 @@
         FL[1 + j, 4] = coarse_load(1, 2 * j)
         mean_coefs(1 + j)
 
-    def coefs_copy(d, arriving):
+    def coefs_copy(e, d, arriving):
         return pltpu.make_async_remote_copy(
             src_ref=FL.at[pl.ds(1, 2)],
             dst_ref=CF.at[pl.ds(2 * (WIDE + d if arriving else WIDE - d), 2)],
-            send_sem=cf_send.at[WIDE + d],
+            send_sem=cf_send.at[e // 4, WIDE + d],
             recv_sem=cf_recv.at[WIDE + d if arriving else WIDE - d],
-            device_id=device(m, t + d),
+            device_id=device(coefs_from(m, d) if arriving else e, t + d),
             device_id_type=MESH,
         )
 
@@ -351,17 +432,33 @@
         for q in range(2):
             CF[2 * WIDE + q] = FL[1 + q]
 
-        def send(d):
-            @pl.when(d != 0)
+    def send_coefs(e, act):
+        def body(i, carry):
+            d = i - WIDE
+
+            @pl.when(jnp.logical_and(gives_coefs(e, d), inside(t + d)))
             def _():
-                coefs_copy(d, False).start()
-
-        over_window(reach, send)
-
-    arrive((0,))
-    both_sides(0, 0)
-    both_sides(1, 1)
-    arrive((1, 2, 3))
+                act(coefs_copy(e, d, False))
+
+            return carry
+
+        lax.fori_loop(0, 2 * WIDE + 1, body, 0)
+
+    arrive((1,))
+    for s in range(2):
+
+        @pl.when(has[s])
+        def _():
+            to_sibling(s, False).start()
+
+    arrive((2,))
+
+    for s in range(2):
+
+        @pl.when(has[s])
+        def _():
+            to_sibling(s, True).wait_recv()
+
     for s in range(2):
 
         @pl.when(has[s])
@@ -372,11 +469,28 @@
                 spread_load(2 - 2 * s, q + 2 * s, r)
             FL[3 - 3 * s, 4] = coarse_load(2 - 2 * s, 2 * s)
             mean_coefs(3 - 3 * s)
-            GU[0, 4 - 3 * s, pl.ds(PAD, CY), :] = mean_rows(0, 7 - 6 * s)
-
+
+    arrive((0,))
+    send_coefs(3, lambda copy: copy.start())
+    both_sides(0, 0)
+    both_sides(1, 1)
+    arrive((3,))
     both_sides(0, -1)
     both_sides(1, 0)
     both_sides(2, 1)
+    for s in range(2):
+
+        @pl.when(has[s])
+        def _():
+            GU[0, 4 - 3 * s, pl.ds(PAD, CY), :] = mean_rows(0, 7 - 6 * s)
+
+    for s in range(2):
+
+        @pl.when(relays[s])
+        def _():
+            for item in (5, 6):
+                by_relay(item, s, 1).wait_recv()
+                by_relay(item, s, 2).start()
 
     arrive((4,))
     for j in (1, 2):
@@ -393,7 +507,7 @@
     for j in (1, 2):
         GG[j - 1] = coarse_step(GU, 1, 1 + j, GC, FL, j)
 
-    arrive((5,))
+    arrive((5, 6))
     both_sides(1, -2)
     both_sides(1, -1)
     both_sides(2, -1)
@@ -425,6 +539,8 @@
     def _():
         send_block(OWN)
 
+    send_coefs(7, lambda copy: copy.start())
+
     def forward(j, tm):
         return pltpu.make_async_remote_copy(
             src_ref=GCB.at[j],
@@ -437,7 +553,7 @@
 
     @pl.when(lead)
     def _():
-        over_window(reach, lambda d: pl.when(d != 0)(lambda: coefs_copy(d, True).wait_recv()))
+        over_window(count, lambda d: pl.when(d != 0)(lambda: coefs_copy(0, d, True).wait_recv()))
 
         def prepare(r, carry):
             combine(CF, CC, r)
@@ -527,17 +643,20 @@
     for copy in stores:
         copy.start()
 
-    for item in range(6):
-        for s in range(2):
-
-            @pl.when(sends[s])
-            def _():
-                halo(item, s, False).wait_send()
+    each_send(lambda copy: copy.wait_send())
+    for s in range(2):
+
+        @pl.when(relays[s])
+        def _():
+            for item in (5, 6):
+                by_relay(item, s, 2).wait_send()
+
+        @pl.when(has[s])
+        def _():
+            to_sibling(s, False).wait_send()
 
     @pl.when(lead)
     def _():
-        over_window(reach, lambda d: pl.when(d != 0)(lambda: coefs_copy(d, False).wait_send()))
-
         def handed(j, carry):
             forward(j, first + 1 + j).wait_send()
             return carry
@@ -552,21 +671,21 @@
     def _():
         sent_block(SEND)
 
+    send_coefs(3, lambda copy: copy.wait_send())
+    send_coefs(7, lambda copy: copy.wait_send())
     for copy in stores:
         copy.wait()
 
 
 def shards(initial_states, material, conductivity, dispersivity, freundlich_k, freundlich_n, surface_load):
-    smem = pl.BlockSpec(memory_space=pltpu.SMEM)
-    anywhere = pl.BlockSpec(memory_space=pl.ANY)
-    vmem = pl.BlockSpec(memory_space=pltpu.VMEM)
+    hbm = pl.BlockSpec(memory_space=pltpu.HBM)
     block = (CY, HALF)
     dma = pltpu.SemaphoreType.DMA
     return pl.pallas_call(
         kernel,
         out_shape=jax.ShapeDtypeStruct(initial_states.shape, F32),
-        in_specs=[smem] * 4 + [vmem, anywhere, anywhere],
-        out_specs=anywhere,
+        in_specs=[hbm] * 7,
+        out_specs=hbm,
         scratch_shapes=[
             pltpu.VMEM((5, 10, 2, FY + 2 * PAD, HALF), F32),
             pltpu.VMEM((8, 2, FY, HALF), jnp.int32),
@@ -586,10 +705,18 @@
             pltpu.VMEM((4, 2) + block, F32),
             pltpu.VMEM((2,) + block, F32),
             pltpu.VMEM((4, 2, FY, HALF), F32),
+            pltpu.VMEM((4, FY), F32),
+            pltpu.SMEM((4, MATS), F32),
+            pltpu.VMEM((2, 2, FY, HALF), F32),
             dma((4,)),
-            dma((6, 2)),
-            dma((6, 2)),
-            dma((2 * WIDE + 1,)),
+            dma((5,)),
+            dma((7, 2)),
+            dma((7, 2)),
+            dma((2,)),
+            dma((2,)),
+            dma((2,)),
+            dma((2,)),
+            dma((2, 2 * WIDE + 1)),
             dma((2 * WIDE + 1,)),
             dma((2 * WIDE + 1,)),
             dma((4, 2 * WIDE + 1)),
@@ -597,7 +724,7 @@
             dma((1,)),
         ],
         compiler_params=pltpu.CompilerParams(
-            collective_id=0, has_side_effects=True, vmem_limit_bytes=40 * 1024 * 1024
+            collective_id=0, has_side_effects=True, vmem_limit_bytes=63 * 1024 * 1024
         ),
     )(conductivity, dispersivity, freundlich_k, freundlich_n, surface_load, initial_states, material)
 

time: 73.7 us -> 57.6 us (0.78)
  Pallas kernels: 67.6 us -> 55.8 us
  local copies, waits for them, and re-layouts: 5.9 us -> 1.67 us
    pallas_call x1, Pallas kernels: 67.6 us -> 55.8 us  [shards(): pl.pallas_call(kernel, out_shape=jax.ShapeDtypeStruct(initial_states.shap...]
    unnamed x15 -> x1, local copies, waits for them, and re-layouts: 5.9 us -> 1.67 us
where the time goes in v2:
time: 57.6 us; the launch traced here: 57.4 us
  Pallas kernels  55.8 us (97%)
  local copies, waits for them, and re-layouts  1.67 us (3%)
    pallas_call x1, Pallas kernels, shards(): pl.pallas_call(kernel, out_shape=jax.ShapeDtypeStruct(initial_states.shap...  55.8 us
    unnamed x1, local copies, waits for them, and re-layouts  1.67 us

profile of v2, /device:TPU:89, one launch (start us, length us, event | category | flops | bytes accessed | tf_op | source)
XLA Modules:
  0.0 57.4 jit_solution(17305345003805881353)
XLA Ops:
  0.0 55.8 %shard_map.73 = f32[1,4,64,256]{3,2,1,0:T(8,128)} custom-call(f32[12]{0:T(128)} %cond.1, f32[12]{0:T(128)} %disp.1, f32[12]{0:T(128)} %fk.1, f32[12]{0:T(128)} %fn.1, f32[4,64]{1,0:T(4,128)} %load.1, f32[1,4,64,256]{3,2,1,0:T(8,128)} %init.1, s32[4,64,256]{2,1,0:T(8,128)} %mat.1), custom_call_target="tpu_custom_call" | custom-call | tf_op jit(solution)/shard_map/pallas_call | solution.py:684
  55.8 1.7 %copy.9 = f32[1,4,64,256]{3,2,1,0:T(8,128)} copy(f32[1,4,64,256]{3,2,1,0:T(8,128)} %shard_map.73) | data formatting | bytes 524288

commit v3 on v2

v3 whole, which is shorter than its diff:
```python
import jax
import jax.numpy as jnp
from jax import lax
from jax.experimental import pallas as pl
from jax.experimental.pallas import tpu as pltpu
from jax.sharding import PartitionSpec as P

MESH = pl.DeviceIdType.MESH
F32 = jnp.float32
MATS = 12
TILES = 32
HALF = 128
FY = 64
CY = 32
PAD = 8
URGENT = 4
LAST = 7
BREAK = 2
LONGEST = max(BREAK, LAST - BREAK)
PAIRS = (LONGEST + 1) // 2
WIDE = 2 * PAIRS
SLOTS = 2 * WIDE + 2
COEFS_FROM = ((3, 5, 4, 4), (6, 4, 0, 1))


def lane(rows):
    return lax.broadcasted_iota(jnp.int32, (rows, HALF), 1)


def roll(value, shift):
    return pltpu.roll(value, shift, 1)


def gather(value, index):
    return jnp.take_along_axis(value, index, axis=1)


def update(um, u0, up, ym, yp, zm, zp, a, b, c, d, kn, n1):
    flux = a * ((up + zp) + (ym + yp)) + b * um + c * zm - d * u0
    power = jnp.exp2(n1 * jnp.log2(jnp.abs(u0) + 1.0))
    return u0 + flux / (1.0 + kn * power)


def squeeze_lanes(low, high):
    rows = low.shape[0]
    at = lane(rows)
    index = (2 * at) % HALF
    low = low + roll(low, HALF - 1)
    high = high + roll(high, HALF - 1)
    return jnp.where(at < HALF // 2, gather(low, index), gather(high, index))


def kernel(
    cond, disp, fk, fn, load, init, mat, out,
    U, M, C, L, LD, FL, GC, GL, GU, GG, OWN, CARRY, W, CF, CC, CL, RD, GCB, FWB, UP,
    LIN, TAB, in_sem, small_sem, halo_send, halo_recv, sib_send, sib_recv, cf_send, cf_recv, s_send, s_recv, c_send, c_recv, fw_send, fw_recv,
):
    m = lax.axis_index("tm")
    t = lax.axis_index("tile")

    def device(tm, tile):
        return {"tm": tm, "tile": tile}

    def inside(tile):
        return jnp.logical_and(tile >= 0, tile < TILES)

    base = t - t % 2

    def leader_of(base):
        return base + 1 - (base % 4) // 2

    head = jnp.where(m <= BREAK, BREAK, LAST)
    lead = jnp.logical_and(m == head, t == leader_of(base))
    first = jnp.where(m <= BREAK, 0, BREAK)
    count = head - first
    place = m - first
    width = head - m

    def both(a, b):
        return jnp.logical_and(a, b)

    def reaches(base, width):
        return both(both(base >= 0, base < TILES), both(base - width <= t, t <= base + 1 + width))

    def coefs_from(e, pairs):
        value = COEFS_FROM[e][PAIRS]
        for i in range(PAIRS):
            value = jnp.where(jnp.abs(pairs) == i, COEFS_FROM[e][i], value)
        return value

    def gives_coefs(e, pairs):
        to = base + 2 * pairs
        return both(both(reaches(to, (BREAK, LAST - BREAK)[e]), m == coefs_from(e, pairs)), t != leader_of(to))

    def gives_block(pairs):
        to = base + 2 * pairs
        return both(both(m < LAST, reaches(to, width)), jnp.logical_or(m < head, t != leader_of(to)))

    x = t % 4
    core = m % 2
    sibling = m + 1 - 2 * core
    far = (x == 0, x == 3)
    has = (t < TILES - 1, t > 0)

    loads = []
    for h in range(2):
        loads.append(pltpu.make_async_copy(mat.at[:, :, pl.ds(HALF * h, HALF)], M.at[pl.ds(2, 4), h], in_sem.at[h]))
    for h in range(2):
        loads.append(
            pltpu.make_async_copy(
                init.at[0, :, :, pl.ds(HALF * h, HALF)], U.at[0, pl.ds(3, 4), h, pl.ds(PAD, FY), :], in_sem.at[2 + h]
            )
        )
    small = [pltpu.make_async_copy(load, LIN, small_sem.at[0])]
    for i, ref in enumerate((cond, disp, fk, fn)):
        small.append(pltpu.make_async_copy(ref, TAB.at[i], small_sem.at[1 + i]))
    for copy in loads + small:
        copy.start()

    barrier = pltpu.get_barrier_semaphore()

    def greet(tm, tile, when):
        @pl.when(jnp.logical_and(when, inside(tile)))
        def _():
            pl.semaphore_signal(barrier, inc=1, device_id=device(tm, tile), device_id_type=MESH)

    greet(m, t - 1, m >= 0)
    greet(m, t + 1, m >= 0)
    greet(sibling, t, m >= 0)

    def needs(i, width):
        return both(i >= WIDE - width, i <= WIDE + 1 + width)

    @pl.when(lead)
    def _():
        def greet_slot(i, carry):
            tile = base - WIDE + i
            pairs = PAIRS - i // 2
            for e in range(2):
                greet(
                    coefs_from(e, pairs), tile, both(m == (BREAK, LAST)[e], both(needs(i, count), tile != t))
                )
            for j in range(LONGEST):
                exists = jnp.logical_or(both(m == BREAK, j <= BREAK), both(m == LAST, both(j > 0, j < count)))
                other = jnp.logical_or(first + j < m, tile != t)
                greet(first + j, tile, both(both(exists, other), needs(i, count - j)))
            return carry

        lax.fori_loop(0, SLOTS, greet_slot, 0)

        @pl.when(m == LAST)
        def _():
            def greet_pair(i, carry):
                to = base + 2 * (i - PAIRS)
                greet(BREAK, leader_of(to), inside(to))
                return carry

            lax.fori_loop(0, 2 * PAIRS + 1, greet_pair, 0)

    greet(head, leader_of(base), both(jnp.logical_not(lead), m > 0))

    def add_pair(i, total):
        pairs = i - PAIRS
        for e in range(2):
            total = total + jnp.where(gives_coefs(e, pairs), 1, 0)
        total = total + jnp.where(gives_block(pairs), 1, 0)
        return total + jnp.where(both(both(lead, m == BREAK), inside(base + 2 * pairs)), 1, 0)

    expected = 1 + jnp.where(t > 0, 1, 0) + jnp.where(t < TILES - 1, 1, 0) + jnp.where(lead, 2 * count - 1, 0)
    expected = expected + lax.fori_loop(0, 2 * PAIRS + 1, add_pair, 0)

    rows = pl.ds(PAD, FY)

    def halo(item, s, arriving):
        src, dst = (
            (U.at[0, 3 + 3 * s, :, rows, :], U.at[0, 7 - 5 * s, :, rows, :]),
            (M.at[2 + 3 * s + core * (1 - 2 * s)], M.at[6 - 5 * s + core * (1 - 2 * s)]),
            (L.at[1], L.at[2 - 2 * s]),
            (U.at[0, 4 + s, :, rows, :], U.at[0, 8 - 7 * s, :, rows, :]),
            (GU.at[0, 3 - s, pl.ds(PAD, CY), :], GU.at[0, 5 - 5 * s, pl.ds(PAD, CY), :]),
            (U.at[1, 4, :, rows, :], U.at[1, 8 - 8 * s, :, rows, :]),
            (U.at[1, 5, :, rows, :], U.at[1, 9 - 8 * s, :, rows, :]),
        )[item]
        toward = 2 * s - 1
        return pltpu.make_async_remote_copy(
            src_ref=src,
            dst_ref=dst,
            send_sem=halo_send.at[item, s],
            recv_sem=halo_recv.at[item, s],
            device_id=device(m, t - toward if arriving else t + toward),
            device_id_type=MESH,
        )

    def to_sibling(s, arriving):
        place = 6 - 5 * s + (1 - core if arriving else core) * (1 - 2 * s)
        return pltpu.make_async_remote_copy(
            src_ref=M.at[place],
            dst_ref=M.at[place],
            send_sem=sib_send.at[s],
            recv_sem=sib_recv.at[s],
            device_id=device(sibling, t),
            device_id_type=MESH,
        )

    sends = (t > 0, t < TILES - 1)

    def send_across(items, when, act):
        for s in range(2):

            @pl.when(jnp.logical_and(when, jnp.logical_and(sends[s], far[s])))
            def _():
                for item in items:
                    act(halo(item, s, False))

    def send_along(items, act):
        for item in items:
            for s in range(2):

                @pl.when(jnp.logical_and(sends[s], jnp.logical_not(far[s])))
                def _():
                    act(halo(item, s, False))

    every = (1, 2, 0, 3, 4, 5, 6)
    urgent = m < URGENT

    def arrive(items):
        for item in items:
            for s in range(2):

                @pl.when(has[s])
                def _():
                    halo(item, s, True).wait_recv()

    for copy in small[:1] + loads:
        copy.wait()
    L[1] = jnp.zeros((8, HALF), F32)
    L[1, 0:4, 0:FY] = LIN[...]
    pl.semaphore_wait(barrier, expected)
    send_across(every[:4], urgent, lambda copy: copy.start())
    send_along(every[:4], lambda copy: copy.start())

    zero = jnp.zeros((PAD, HALF), F32)

    def blank_fine(i, carry):
        for h in range(2):
            U[i // 10, i % 10, h, pl.ds(0, PAD), :] = zero
            U[i // 10, i % 10, h, pl.ds(PAD + FY, PAD), :] = zero
        return carry

    lax.fori_loop(0, 50, blank_fine, 0)

    def blank_coarse(i, carry):
        for k in range(2):
            W[k, i, pl.ds(0, PAD), :] = zero
            W[k, i, pl.ds(PAD + CY, PAD), :] = zero
        return carry

    lax.fori_loop(0, 2 * SLOTS, blank_coarse, 0)
    for k in range(2):
        for r in range(6):
            GU[k, r, pl.ds(0, PAD), :] = zero
            GU[k, r, pl.ds(PAD + CY, PAD), :] = zero
    for s in range(2):

        @pl.when(jnp.logical_not(has[s]))
        def _():
            def clear(i, carry):
                for h in range(2):
                    U[i // 3, 7 - 7 * s + i % 3, h, pl.ds(PAD, FY), :] = jnp.zeros((FY, HALF), F32)
                return carry

            lax.fori_loop(0, 12, clear, 0)
            for k in range(2):
                for r in range(2):
                    GU[k, 4 - 4 * s + r, pl.ds(PAD, CY), :] = jnp.zeros((CY, HALF), F32)

    @pl.when(lead)
    def _():
        def clear(i, carry):
            @pl.when(jnp.logical_not(inside(base + i - WIDE)))
            def _():
                for q in range(2):
                    for f in range(6):
                        CC[2 * i + q, f] = jnp.zeros((CY, HALF), F32)
                    CL[2 * i + q] = jnp.zeros((CY, HALF), F32)
                    for j in range(LONGEST):
                        RD[j, 2 * i + q] = jnp.zeros((CY, HALF), F32)

            return carry

        lax.fori_loop(0, SLOTS, clear, 0)

    at = lane(8)
    tables = []
    for copy in small[1:]:
        copy.wait()
    for k in range(4):
        table = jnp.zeros((8, HALF), F32)
        for i in range(MATS):
            table = jnp.where(at == i, TAB[k, i], table)
        tables.append(table)
    t_cond, t_disp, t_k, t_n = tables
    t_a = t_disp * t_cond
    tables = [t_a, t_a + 0.5 * t_cond, t_a + 0.3 * t_cond, 6.0 * t_a + 0.8 * t_cond, t_k * t_n, t_n - 1.0, t_k]

    def look_up(r):
        for h in range(2):
            index = M[r, h]
            for f, table in enumerate(tables):
                value = gather(jnp.broadcast_to(table[0:1], (FY, HALF)), index)
                if f == 2 and h == 0:
                    value = jnp.where(lane(FY) == 0, 1.0, value)
                C[f, r, h] = value

    def spread_load(s, i, r):
        row = jnp.broadcast_to(L[s, i : i + 1, :], (FY, HALF))
        here = lax.broadcasted_iota(jnp.int32, (FY, HALF), 0) == lane(FY)
        total = jnp.sum(jnp.where(here, row, 0.0), axis=1, keepdims=True)
        LD[r] = jnp.broadcast_to(total, (FY, HALF))

    def coarse_load(rows):
        row = jnp.broadcast_to(rows[0:1] + rows[1:2], (CY, HALF))
        here = lax.broadcasted_iota(jnp.int32, (CY, HALF), 0) == lane(CY) // 2
        total = jnp.sum(jnp.where(here, row, 0.0), axis=1, keepdims=True)
        return jnp.broadcast_to(0.25 * total, (CY, HALF))

    def fine_step(k, r):
        for y in (0, 32):
            rows = pl.ds(PAD + y, 32)
            here = pl.ds(y, 32)
            low, high = U[k, r, 0, rows, :], U[k, r, 1, rows, :]
            at = lane(32)
            back = (roll(low, 1), roll(high, 1))
            ahead = (roll(low, HALF - 1), roll(high, HALF - 1))
            zms = (jnp.where(at == 0, LD[r - 1, here], back[0]), jnp.where(at == 0, back[0], back[1]))
            zps = (jnp.where(at == HALF - 1, ahead[1], ahead[0]), jnp.where(at == HALF - 1, 0.0, ahead[1]))
            for h in range(2):
                U[k + 1, r, h, rows, :] = update(
                    U[k, r - 1, h, rows, :],
                    (low, high)[h],
                    U[k, r + 1, h, rows, :],
                    U[k, r, h, pl.ds(PAD + y - 1, 32), :],
                    U[k, r, h, pl.ds(PAD + y + 1, 32), :],
                    zms[h],
                    zps[h],
                    *[C[f, r - 1, h, here] for f in range(6)],
                )

    def mean_rows(k, r):
        halves = []
        for h in range(2):
            parts = [U[k, r + q, h, pl.ds(PAD + p, CY, stride=2), :] for q in range(2) for p in range(2)]
            halves.append((parts[0] + parts[1]) + (parts[2] + parts[3]))
        return 0.125 * squeeze_lanes(*halves)

    def mean_coefs(j):
        means = []
        for f in (0, 1, 6, 5):
            halves = []
            for h in range(2):
                parts = [C[f, 2 * j + q, h, pl.ds(p, CY, stride=2), :] for q in range(2) for p in range(2)]
                halves.append((parts[0] + parts[1]) + (parts[2] + parts[3]))
            means.append(0.125 * squeeze_lanes(*halves))
        return 0.5 * means[0], 2.0 * (means[1] - means[0]), means[2] * (means[3] + 1.0), means[3]

    def combine(fields, dst, r):
        a, cond, kn, n1 = fields
        dst[r, 0] = a
        dst[r, 1] = a + 0.5 * cond
        dst[r, 2] = jnp.where(lane(CY) == 0, 1.0, a + 0.3 * cond)
        dst[r, 3] = 6.0 * a + 0.8 * cond
        dst[r, 4] = kn
        dst[r, 5] = n1

    def coarse_step(src, k, r, coefs, inflow, place):
        rows = pl.ds(PAD, CY)
        at = lane(CY)
        u0 = src[k, r, rows, :]
        return update(
            src[k, r - 1, rows, :],
            u0,
            src[k, r + 1, rows, :],
            src[k, r, pl.ds(PAD - 1, CY), :],
            src[k, r, pl.ds(PAD + 1, CY), :],
            jnp.where(at == 0, inflow[place], roll(u0, 1)),
            jnp.where(at == HALF - 1, 0.0, roll(u0, HALF - 1)),
            *[coefs[place, f] for f in range(6)],
        )

    for i in range(4):
        spread_load(1, i, 2 + i)

    def own_rows(r, carry):
        look_up(r)
        return carry

    lax.fori_loop(2, 6, own_rows, 0)

    def inner_rows(r, carry):
        fine_step(0, r)
        return carry

    lax.fori_loop(4, 6, inner_rows, 0)
    for j in range(2):
        GU[0, 2 + j, pl.ds(PAD, CY), :] = mean_rows(0, 3 + 2 * j)
    send_across(every[4:], urgent, lambda copy: copy.start())
    send_along(every[4:], lambda copy: copy.start())

    def both_sides(k, near):
        for s in range(2):
            r = 3 + (near if s == 1 else 3 - near)
            if near >= 0:
                fine_step(k, r)
            else:

                @pl.when(has[s])
                def _():
                    fine_step(k, r)

    for q in range(2):
        fields = mean_coefs(1 + q)
        for f in range(4):
            FL[pl.ds((4 * q + f) * CY, CY), :] = fields[f]
        combine(fields, GC, 1 + q)
        GL[1 + q] = coarse_load(L[1, 2 * q : 2 * q + 2, :])
    FL[pl.ds(8 * CY, 8), :] = L[1]

    def coefs_copy(e, pairs):
        to = base + 2 * pairs
        slot = t - to + WIDE
        return pltpu.make_async_remote_copy(
            src_ref=FL,
            dst_ref=CF.at[slot],
            send_sem=cf_send.at[e, PAIRS + pairs],
            recv_sem=cf_recv.at[slot],
            device_id=device((BREAK, LAST)[e], leader_of(to)),
            device_id_type=MESH,
        )

    def coefs_arrive(slot):
        pltpu.make_async_remote_copy(
            src_ref=FL,
            dst_ref=CF.at[slot],
            send_sem=cf_send.at[0, 0],
            recv_sem=cf_recv.at[slot],
            device_id=device(sibling, t),
            device_id_type=MESH,
        ).wait_recv()

    def over_pairs(gives, act):
        def body(i, carry):
            @pl.when(gives(i - PAIRS))
            def _():
                act(i - PAIRS)

            return carry

        lax.fori_loop(0, 2 * PAIRS + 1, body, 0)

    def over_slots(width, act):
        def body(i, carry):
            @pl.when(inside(base - WIDE + i))
            def _():
                act(i)

            return carry

        lax.fori_loop(WIDE - width, WIDE + 2 + width, body, 0)

    def send_coefs(e, act):
        over_pairs(lambda pairs: gives_coefs(e, pairs), lambda pairs: act(coefs_copy(e, pairs)))

    send_coefs(0, lambda copy: copy.start())
    send_across(every, jnp.logical_not(urgent), lambda copy: copy.start())

    arrive((1,))
    for s in range(2):

        @pl.when(has[s])
        def _():
            to_sibling(s, False).start()

    arrive((2,))

    for s in range(2):

        @pl.when(has[s])
        def _():
            to_sibling(s, True).wait_recv()

    for s in range(2):

        @pl.when(has[s])
        def _():
            for q in range(2):
                r = 6 - 6 * s + q
                look_up(r)
                spread_load(2 - 2 * s, q + 2 * s, r)
            GL[3 - 3 * s] = coarse_load(L[2 - 2 * s, 2 * s : 2 * s + 2, :])
            combine(mean_coefs(3 - 3 * s), GC, 3 - 3 * s)

    arrive((0,))
    both_sides(0, 0)
    both_sides(1, 1)
    arrive((3,))
    send_coefs(1, lambda copy: copy.start())
    both_sides(0, -1)
    both_sides(1, 0)
    both_sides(2, 1)
    for s in range(2):

        @pl.when(has[s])
        def _():
            GU[0, 4 - 3 * s, pl.ds(PAD, CY), :] = mean_rows(0, 7 - 6 * s)

    arrive((4,))
    for j in (1, 2):
        GU[1, 1 + j, pl.ds(PAD, CY), :] = coarse_step(GU, 0, 1 + j, GC, GL, j)
    for s in range(2):

        @pl.when(has[s])
        def _():
            j = 3 - 3 * s
            GU[1, 1 + j, pl.ds(PAD, CY), :] = coarse_step(GU, 0, 1 + j, GC, GL, j)

    for j in (1, 2):
        GG[j - 1] = coarse_step(GU, 1, 1 + j, GC, GL, j)

    arrive((5, 6))
    both_sides(1, -2)
    both_sides(1, -1)
    both_sides(2, -1)
    both_sides(2, 0)
    both_sides(3, 0)
    both_sides(3, 1)

    for j in range(2):
        mean = mean_rows(4, 3 + 2 * j)
        OWN[j] = jnp.where(m == 0, mean, mean - GG[j])

    def block_copy(pairs):
        to = base + 2 * pairs
        slot = t - to + WIDE
        return pltpu.make_async_remote_copy(
            src_ref=OWN,
            dst_ref=RD.at[place, pl.ds(2 * slot, 2)],
            send_sem=s_send.at[PAIRS + pairs],
            recv_sem=s_recv.at[place, slot],
            device_id=device(head, leader_of(to)),
            device_id_type=MESH,
        )

    def block_arrives(j, slot):
        pltpu.make_async_remote_copy(
            src_ref=OWN,
            dst_ref=RD.at[j, pl.ds(2 * slot, 2)],
            send_sem=s_send.at[0],
            recv_sem=s_recv.at[j, slot],
            device_id=device(sibling, t),
            device_id_type=MESH,
        ).wait_recv()

    over_pairs(gives_block, lambda pairs: block_copy(pairs).start())

    def carry_copy(pairs):
        to = base + 2 * pairs
        return pltpu.make_async_remote_copy(
            src_ref=CARRY,
            dst_ref=RD.at[0, pl.ds(2 * (WIDE - 2 * pairs), 4)],
            send_sem=c_send.at[PAIRS + pairs],
            recv_sem=c_recv.at[PAIRS - pairs],
            device_id=device(LAST, leader_of(to)),
            device_id_type=MESH,
        )

    def carry_arrives(pairs):
        pltpu.make_async_remote_copy(
            src_ref=CARRY,
            dst_ref=RD.at[0, pl.ds(2 * (WIDE + 2 * pairs), 4)],
            send_sem=c_send.at[0],
            recv_sem=c_recv.at[PAIRS + pairs],
            device_id=device(sibling, t),
            device_id_type=MESH,
        ).wait_recv()

    def carry_pair(pairs):
        return inside(base + 2 * pairs)

    def forward(j, q):
        return pltpu.make_async_remote_copy(
            src_ref=GCB.at[j, pl.ds(2 * q, 2)],
            dst_ref=FWB,
            send_sem=fw_send.at[j, q],
            recv_sem=fw_recv.at[0],
            device_id=device(first + 1 + j, base + q),
            device_id_type=MESH,
        )

    def forwards(j, act):
        for q in range(2):

            @pl.when(jnp.logical_or(j < count - 1, base + q != t))
            def _():
                act(forward(j, q))

    @pl.when(lead)
    def _():
        def prepare(i):
            @pl.when(base - WIDE + i != t)
            def _():
                coefs_arrive(i)

            @pl.when(base - WIDE + i == t)
            def _():
                CF[i] = FL[...]

            for q in range(2):
                combine([CF[i, pl.ds((4 * q + f) * CY, CY), :] for f in range(4)], CC, 2 * i + q)
                CL[2 * i + q] = coarse_load(CF[i, pl.ds(8 * CY + 2 * q, 2), :])

        over_slots(count, prepare)

        def chain(j, carry):
            @pl.when(jnp.logical_or(m == BREAK, j > 0))
            def _():
                over_slots(count - j, lambda i: block_arrives(j, i))

            @pl.when(both(m == LAST, j == 0))
            def _():
                over_pairs(carry_pair, carry_arrives)

            w = count - 1 - j

            @pl.when(j == 0)
            def _():
                def lay(r, carry):
                    W[0, r, pl.ds(PAD, CY), :] = RD[0, r]
                    return carry

                lax.fori_loop(2 * (WIDE - count), 2 * (WIDE + count + 2), lay, 0)

            @pl.when(j > 0)
            def _():
                def add(r, carry):
                    W[0, r, pl.ds(PAD, CY), :] = W[0, r, pl.ds(PAD, CY), :] + RD[j, r]
                    return carry

                lax.fori_loop(2 * (WIDE - w - 1), 2 * (WIDE + w + 3), add, 0)

            def step(k, start, rows):
                for q in range(rows):
                    W[1 - k, start + q, pl.ds(PAD, CY), :] = coarse_step(W, k, start + q, CC, CL, start + q)

            def one(i, carry):
                step(0, 2 * (WIDE - w) - 1 + 4 * i, 4)
                return carry

            lax.fori_loop(0, w + 1, one, 0)
            step(0, 2 * (WIDE + w) + 3, 2)

            def two(i, carry):
                step(1, 2 * (WIDE - w) + 4 * i, 4)
                return carry

            lax.fori_loop(0, w + 1, two, 0)
            for q in range(4):
                GCB[j, q] = W[0, 2 * WIDE + q, pl.ds(PAD, CY), :]
            forwards(j, lambda copy: copy.start())
            return carry

        lax.fori_loop(0, count, chain, 0)

        own = t - base

        @pl.when(m == BREAK)
        def _():
            block_arrives(BREAK, WIDE + 1 - own)
            for q in range(2):
                RD[BREAK, 2 * WIDE + 2 * own + q] = OWN[q]
            for q in range(4):
                CARRY[q] = GCB[BREAK - 1, q] + RD[BREAK, 2 * WIDE + q]
            over_pairs(carry_pair, lambda pairs: carry_copy(pairs).start())

        for q in range(2):
            FWB[q] = GCB[count - 1, 2 * own + q]

    @pl.when(m == 0)
    def _():
        for q in range(2):
            FWB[q] = GG[q]

    @pl.when(jnp.logical_not(jnp.logical_or(lead, m == 0)))
    def _():
        forward(0, 0).wait_recv()

    for j in range(2):
        shift = FWB[j] - GG[j]
        for h in range(2):
            wide = gather(shift, lane(CY) // 2 + 64 * h)
            for p in range(2):
                UP[j, h, pl.ds(p, CY, stride=2), :] = wide
            for q in range(2):
                out[0, 2 * j + q, :, HALF * h : HALF * h + HALF] = U[4, 3 + 2 * j + q, h, rows, :] + UP[j, h]

    send_across(every, m >= 0, lambda copy: copy.wait_send())
    send_along(every, lambda copy: copy.wait_send())
    for s in range(2):

        @pl.when(has[s])
        def _():
            to_sibling(s, False).wait_send()

    @pl.when(lead)
    def _():
        def handed(j, carry):
            forwards(j, lambda copy: copy.wait_send())
            return carry

        lax.fori_loop(0, count, handed, 0)

        @pl.when(m == BREAK)
        def _():
            over_pairs(carry_pair, lambda pairs: carry_copy(pairs).wait_send())

    over_pairs(gives_block, lambda pairs: block_copy(pairs).wait_send())
    for e in range(2):
        send_coefs(e, lambda copy: copy.wait_send())


def shards(initial_states, material, conductivity, dispersivity, freundlich_k, freundlich_n, surface_load):
    hbm = pl.BlockSpec(memory_space=pltpu.HBM)
    block = (CY, HALF)
    dma = pltpu.SemaphoreType.DMA
    return pl.pallas_call(
        kernel,
        out_shape=pltpu.VMEM(initial_states.shape, F32),
        in_specs=[hbm] * 7,
        out_specs=pl.BlockSpec(memory_space=pltpu.VMEM),
        scratch_shapes=[
            pltpu.VMEM((5, 10, 2, FY + 2 * PAD, HALF), F32),
            pltpu.VMEM((8, 2, FY, HALF), jnp.int32),
            pltpu.VMEM((7, 8, 2, FY, HALF), F32),
            pltpu.VMEM((3, 8, HALF), F32),
            pltpu.VMEM((8, FY, HALF), F32),
            pltpu.VMEM((8 * CY + 8, HALF), F32),
            pltpu.VMEM((4, 6) + block, F32),
            pltpu.VMEM((4,) + block, F32),
            pltpu.VMEM((2, 6, CY + 2 * PAD, HALF), F32),
            pltpu.VMEM((2,) + block, F32),
            pltpu.VMEM((2,) + block, F32),
            pltpu.VMEM((4,) + block, F32),
            pltpu.VMEM((2, 2 * SLOTS, CY + 2 * PAD, HALF), F32),
            pltpu.VMEM((SLOTS, 8 * CY + 8, HALF), F32),
            pltpu.VMEM((2 * SLOTS, 6) + block, F32),
            pltpu.VMEM((2 * SLOTS,) + block, F32),
            pltpu.VMEM((LONGEST, 2 * SLOTS) + block, F32),
            pltpu.VMEM((LONGEST, 4) + block, F32),
            pltpu.VMEM((2,) + block, F32),
            pltpu.VMEM((2, 2, FY, HALF), F32),
            pltpu.VMEM((4, FY), F32),
            pltpu.SMEM((4, MATS), F32),
            dma((4,)),
            dma((5,)),
            dma((7, 2)),
            dma((7, 2)),
            dma((2,)),
            dma((2,)),
            dma((2, 2 * PAIRS + 1)),
            dma((SLOTS,)),
            dma((2 * PAIRS + 1,)),
            dma((LONGEST, SLOTS)),
            dma((2 * PAIRS + 1,)),
            dma((2 * PAIRS + 1,)),
            dma((LONGEST, 2)),
            dma((1,)),
        ],
        compiler_params=pltpu.CompilerParams(
            collective_id=0, has_side_effects=True, vmem_limit_bytes=63 * 1024 * 1024
        ),
    )(conductivity, dispersivity, freundlich_k, freundlich_n, surface_load, initial_states, material)


def solution(mesh):
    in_specs = (
        P("tm", "tile", None, None),
        P("tile", None, None),
        P(),
        P(),
        P(),
        P(),
        P("tile", None),
    )
    out_specs = P("tm", "tile", None, None)
    return jax.shard_map(shards, mesh=mesh, in_specs=in_specs, out_specs=out_specs, check_vma=False)
```

time: 57.6 us -> 51.3 us (0.89)
  Pallas kernels: 55.8 us -> 50.5 us
  local copies, waits for them, and re-layouts: 1.67 us -> 0.71 us
    pallas_call x1, Pallas kernels: 55.8 us -> 50.5 us  [shards(): pl.pallas_call(kernel, out_shape=pltpu.VMEM(initial_states.shape, F32), i...]
    unnamed x1, local copies, waits for them, and re-layouts: 1.67 us -> 0.71 us
where the time goes in v3:
time: 51.3 us; the launch traced here: 51.2 us
  Pallas kernels  50.5 us (98%)
  local copies, waits for them, and re-layouts  0.71 us (1%)
    pallas_call x1, Pallas kernels, shards(): pl.pallas_call(kernel, out_shape=pltpu.VMEM(initial_states.shape, F32), i...  50.5 us

profile of v3, /device:TPU:89, one launch (start us, length us, event | category | flops | bytes accessed | tf_op | source)
XLA Modules:
  0.0 51.2 jit_solution(16222867499408605448)
XLA Ops:
  0.0 50.5 %shard_map.73 = f32[1,4,64,256]{3,2,1,0:T(8,128)S(1)} custom-call(f32[12]{0:T(128)} %cond.1, f32[12]{0:T(128)} %disp.1, f32[12]{0:T(128)} %fk.1, f32[12]{0:T(128)} %fn.1, f32[4,64]{1,0:T(4,128)} %load.1, f32[1,4,64,256]{3,2,1,0:T(8,128)} %init.1, s32[4,64,256]{2,1,0:T(8,128)} %mat.1), custom_call_target="tpu_custom_call" | custom-call | tf_op jit(solution)/shard_map/pallas_call | solution.py:734
  50.5 0.7 %copy.9 = f32[1,4,64,256]{3,2,1,0:T(8,128)} copy(f32[1,4,64,256]{3,2,1,0:T(8,128)S(1)} %shard_map.73) | data formatting | bytes 524288

commit v4 on v3

--- a/solution.py
+++ b/solution.py
@@ -15,12 +15,12 @@
 PAD = 8
 URGENT = 4
 LAST = 7
-BREAK = 2
+BREAK = 3
 LONGEST = max(BREAK, LAST - BREAK)
 PAIRS = (LONGEST + 1) // 2
 WIDE = 2 * PAIRS
 SLOTS = 2 * WIDE + 2
-COEFS_FROM = ((3, 5, 4, 4), (6, 4, 0, 1))
+COEFS_FROM = ((2, 5, 4), (6, 4, 1))
 
 
 def lane(rows):

time: 51.3 us -> 46.7 us (0.910)
  Pallas kernels: 50.5 us -> 45.9 us
    pallas_call x1, Pallas kernels: 50.5 us -> 45.9 us  [shards(): pl.pallas_call(kernel, out_shape=pltpu.VMEM(initial_states.shape, F32), i...]
where the time goes in v4:
time: 46.7 us; the launch traced here: 46.6 us
  Pallas kernels  45.9 us (98%)
  local copies, waits for them, and re-layouts  0.71 us (2%)
    pallas_call x1, Pallas kernels, shards(): pl.pallas_call(kernel, out_shape=pltpu.VMEM(initial_states.shape, F32), i...  45.9 us

profile of v4, /device:TPU:89, one launch (start us, length us, event | category | flops | bytes accessed | tf_op | source)
XLA Modules:
  0.0 46.6 jit_solution(9161023611467917329)
XLA Ops:
  0.0 45.9 %shard_map.73 = f32[1,4,64,256]{3,2,1,0:T(8,128)S(1)} custom-call(f32[12]{0:T(128)} %cond.1, f32[12]{0:T(128)} %disp.1, f32[12]{0:T(128)} %fk.1, f32[12]{0:T(128)} %fn.1, f32[4,64]{1,0:T(4,128)} %load.1, f32[1,4,64,256]{3,2,1,0:T(8,128)} %init.1, s32[4,64,256]{2,1,0:T(8,128)} %mat.1), custom_call_target="tpu_custom_call" | custom-call | tf_op jit(solution)/shard_map/pallas_call | solution.py:734
  45.9 0.7 %copy.9 = f32[1,4,64,256]{3,2,1,0:T(8,128)} copy(f32[1,4,64,256]{3,2,1,0:T(8,128)S(1)} %shard_map.73) | data formatting | bytes 524288

commit v5 on v4

--- a/solution.py
+++ b/solution.py
@@ -128,34 +128,33 @@
     greet(m, t + 1, m >= 0)
     greet(sibling, t, m >= 0)
 
-    def needs(i, width):
-        return both(i >= WIDE - width, i <= WIDE + 1 + width)
-
-    @pl.when(lead)
-    def _():
-        def greet_slot(i, carry):
-            tile = base - WIDE + i
-            pairs = PAIRS - i // 2
-            for e in range(2):
-                greet(
-                    coefs_from(e, pairs), tile, both(m == (BREAK, LAST)[e], both(needs(i, count), tile != t))
-                )
-            for j in range(LONGEST):
-                exists = jnp.logical_or(both(m == BREAK, j <= BREAK), both(m == LAST, both(j > 0, j < count)))
-                other = jnp.logical_or(first + j < m, tile != t)
-                greet(first + j, tile, both(both(exists, other), needs(i, count - j)))
-            return carry
-
-        lax.fori_loop(0, SLOTS, greet_slot, 0)
-
-        @pl.when(m == LAST)
-        def _():
-            def greet_pair(i, carry):
-                to = base + 2 * (i - PAIRS)
-                greet(BREAK, leader_of(to), inside(to))
-                return carry
-
-            lax.fori_loop(0, 2 * PAIRS + 1, greet_pair, 0)
+    for e, (slice_, start) in enumerate(((BREAK, 0), (LAST, BREAK))):
+
+        @pl.when(both(lead, m == slice_))
+        def _():
+            reach = slice_ - start
+            for j in range(reach):
+                if j == 0 and e == 1:
+
+                    def greet_pair(i, carry):
+                        to = base + 2 * (i - PAIRS)
+                        greet(BREAK, leader_of(to), m >= 0)
+                        return carry
+
+                    lax.fori_loop(0, 2 * PAIRS + 1, greet_pair, 0)
+                else:
+
+                    def greet_tile(i, carry):
+                        greet(start + j, base + i - (reach - j), m >= 0)
+                        return carry
+
+                    lax.fori_loop(0, 2 + 2 * (reach - j), greet_tile, 0)
+            for pairs in range(-PAIRS, PAIRS + 1):
+                for i in (2 * pairs, 2 * pairs + 1):
+                    if -reach <= i <= 1 + reach:
+                        greet(COEFS_FROM[e][abs(pairs)], base + i, base + i != t)
+            if e == 0:
+                greet(BREAK, 2 * base + 1 - t, m >= 0)
 
     greet(head, leader_of(base), both(jnp.logical_not(lead), m > 0))
 
@@ -236,7 +235,8 @@
     L[1] = jnp.zeros((8, HALF), F32)
     L[1, 0:4, 0:FY] = LIN[...]
     pl.semaphore_wait(barrier, expected)
-    send_across(every[:4], urgent, lambda copy: copy.start())
+    send_across(every[:2], m >= 0, lambda copy: copy.start())
+    send_across(every[2:4], urgent, lambda copy: copy.start())
     send_along(every[:4], lambda copy: copy.start())
 
     zero = jnp.zeros((PAD, HALF), F32)
@@ -283,6 +283,7 @@
                     for f in range(6):
                         CC[2 * i + q, f] = jnp.zeros((CY, HALF), F32)
                     CL[2 * i + q] = jnp.zeros((CY, HALF), F32)
+                    W[0, 2 * i + q, pl.ds(PAD, CY), :] = jnp.zeros((CY, HALF), F32)
                     for j in range(LONGEST):
                         RD[j, 2 * i + q] = jnp.zeros((CY, HALF), F32)
 
@@ -471,7 +472,6 @@
         over_pairs(lambda pairs: gives_coefs(e, pairs), lambda pairs: act(coefs_copy(e, pairs)))
 
     send_coefs(0, lambda copy: copy.start())
-    send_across(every, jnp.logical_not(urgent), lambda copy: copy.start())
 
     arrive((1,))
     for s in range(2):
@@ -482,6 +482,7 @@
 
     arrive((2,))
 
+    send_across(every[2:], jnp.logical_not(urgent), lambda copy: copy.start())
     for s in range(2):
 
         @pl.when(has[s])
@@ -538,35 +539,45 @@
         mean = mean_rows(4, 3 + 2 * j)
         OWN[j] = jnp.where(m == 0, mean, mean - GG[j])
 
-    def block_copy(pairs):
+    def block_copy(pairs, initial):
         to = base + 2 * pairs
         slot = t - to + WIDE
+        dst = W.at[0, pl.ds(2 * slot, 2), pl.ds(PAD, CY), :] if initial else RD.at[place, pl.ds(2 * slot, 2)]
         return pltpu.make_async_remote_copy(
             src_ref=OWN,
-            dst_ref=RD.at[place, pl.ds(2 * slot, 2)],
+            dst_ref=dst,
             send_sem=s_send.at[PAIRS + pairs],
             recv_sem=s_recv.at[place, slot],
             device_id=device(head, leader_of(to)),
             device_id_type=MESH,
         )
 
-    def block_arrives(j, slot):
+    def block_arrives(j, slot, initial):
         pltpu.make_async_remote_copy(
             src_ref=OWN,
-            dst_ref=RD.at[j, pl.ds(2 * slot, 2)],
+            dst_ref=W.at[0, pl.ds(2 * slot, 2), pl.ds(PAD, CY), :] if initial else RD.at[j, pl.ds(2 * slot, 2)],
             send_sem=s_send.at[0],
             recv_sem=s_recv.at[j, slot],
             device_id=device(sibling, t),
             device_id_type=MESH,
         ).wait_recv()
 
-    over_pairs(gives_block, lambda pairs: block_copy(pairs).start())
+    def each_block(act):
+        @pl.when(m == 0)
+        def _():
+            over_pairs(gives_block, lambda pairs: act(block_copy(pairs, True)))
+
+        @pl.when(m > 0)
+        def _():
+            over_pairs(gives_block, lambda pairs: act(block_copy(pairs, False)))
+
+    each_block(lambda copy: copy.start())
 
     def carry_copy(pairs):
         to = base + 2 * pairs
         return pltpu.make_async_remote_copy(
             src_ref=CARRY,
-            dst_ref=RD.at[0, pl.ds(2 * (WIDE - 2 * pairs), 4)],
+            dst_ref=W.at[0, pl.ds(2 * (WIDE - 2 * pairs), 4), pl.ds(PAD, CY), :],
             send_sem=c_send.at[PAIRS + pairs],
             recv_sem=c_recv.at[PAIRS - pairs],
             device_id=device(LAST, leader_of(to)),
@@ -576,7 +587,7 @@
     def carry_arrives(pairs):
         pltpu.make_async_remote_copy(
             src_ref=CARRY,
-            dst_ref=RD.at[0, pl.ds(2 * (WIDE + 2 * pairs), 4)],
+            dst_ref=W.at[0, pl.ds(2 * (WIDE + 2 * pairs), 4), pl.ds(PAD, CY), :],
             send_sem=c_send.at[0],
             recv_sem=c_recv.at[PAIRS + pairs],
             device_id=device(sibling, t),
@@ -603,6 +614,17 @@
             def _():
                 act(forward(j, q))
 
+    send_across(every, m >= 0, lambda copy: copy.wait_send())
+    send_along(every, lambda copy: copy.wait_send())
+    for s in range(2):
+
+        @pl.when(has[s])
+        def _():
+            to_sibling(s, False).wait_send()
+    each_block(lambda copy: copy.wait_send())
+    for e in range(2):
+        send_coefs(e, lambda copy: copy.wait_send())
+
     @pl.when(lead)
     def _():
         def prepare(i):
@@ -621,9 +643,13 @@
         over_slots(count, prepare)
 
         def chain(j, carry):
-            @pl.when(jnp.logical_or(m == BREAK, j > 0))
-            def _():
-                over_slots(count - j, lambda i: block_arrives(j, i))
+            @pl.when(both(m == BREAK, j == 0))
+            def _():
+                over_slots(count, lambda i: block_arrives(0, i, True))
+
+            @pl.when(j > 0)
+            def _():
+                over_slots(count - j, lambda i: block_arrives(j, i, False))
 
             @pl.when(both(m == LAST, j == 0))
             def _():
@@ -631,38 +657,34 @@
 
             w = count - 1 - j
 
-            @pl.when(j == 0)
-            def _():
-                def lay(r, carry):
-                    W[0, r, pl.ds(PAD, CY), :] = RD[0, r]
+            @pl.when(j > 0)
+            def _():
+                def add(i, carry):
+                    for q in range(4):
+                        r = 2 * (WIDE - w - 1) + 4 * i + q
+                        W[0, r, pl.ds(PAD, CY), :] = W[0, r, pl.ds(PAD, CY), :] + RD[j, r]
                     return carry
 
-                lax.fori_loop(2 * (WIDE - count), 2 * (WIDE + count + 2), lay, 0)
-
-            @pl.when(j > 0)
-            def _():
-                def add(r, carry):
-                    W[0, r, pl.ds(PAD, CY), :] = W[0, r, pl.ds(PAD, CY), :] + RD[j, r]
-                    return carry
-
-                lax.fori_loop(2 * (WIDE - w - 1), 2 * (WIDE + w + 3), add, 0)
+                lax.fori_loop(0, w + 2, add, 0)
 
             def step(k, start, rows):
                 for q in range(rows):
                     W[1 - k, start + q, pl.ds(PAD, CY), :] = coarse_step(W, k, start + q, CC, CL, start + q)
 
-            def one(i, carry):
-                step(0, 2 * (WIDE - w) - 1 + 4 * i, 4)
-                return carry
-
-            lax.fori_loop(0, w + 1, one, 0)
+            def sweep(k, start):
+                def eight(i, carry):
+                    step(k, start + 8 * i, 8)
+                    return carry
+
+                lax.fori_loop(0, jnp.where(w == 3, 2, jnp.where(w == 0, 0, 1)), eight, 0)
+
+                @pl.when(jnp.logical_or(w == 0, w == 2))
+                def _():
+                    step(k, start + 4 * w, 4)
+
+            sweep(0, 2 * (WIDE - w) - 1)
             step(0, 2 * (WIDE + w) + 3, 2)
-
-            def two(i, carry):
-                step(1, 2 * (WIDE - w) + 4 * i, 4)
-                return carry
-
-            lax.fori_loop(0, w + 1, two, 0)
+            sweep(1, 2 * (WIDE - w))
             for q in range(4):
                 GCB[j, q] = W[0, 2 * WIDE + q, pl.ds(PAD, CY), :]
             forwards(j, lambda copy: copy.start())
@@ -674,7 +696,7 @@
 
         @pl.when(m == BREAK)
         def _():
-            block_arrives(BREAK, WIDE + 1 - own)
+            block_arrives(BREAK, WIDE + 1 - own, False)
             for q in range(2):
                 RD[BREAK, 2 * WIDE + 2 * own + q] = OWN[q]
             for q in range(4):
@@ -702,14 +724,6 @@
             for q in range(2):
                 out[0, 2 * j + q, :, HALF * h : HALF * h + HALF] = U[4, 3 + 2 * j + q, h, rows, :] + UP[j, h]
 
-    send_across(every, m >= 0, lambda copy: copy.wait_send())
-    send_along(every, lambda copy: copy.wait_send())
-    for s in range(2):
-
-        @pl.when(has[s])
-        def _():
-            to_sibling(s, False).wait_send()
-
     @pl.when(lead)
     def _():
         def handed(j, carry):
@@ -721,10 +735,6 @@
         @pl.when(m == BREAK)
         def _():
             over_pairs(carry_pair, lambda pairs: carry_copy(pairs).wait_send())
-
-    over_pairs(gives_block, lambda pairs: block_copy(pairs).wait_send())
-    for e in range(2):
-        send_coefs(e, lambda copy: copy.wait_send())
 
 
 def shards(initial_states, material, conductivity, dispersivity, freundlich_k, freundlich_n, surface_load):

time: 46.7 us -> 45.1 us (0.966)
  Pallas kernels: 45.9 us -> 44.1 us
    pallas_call x1, Pallas kernels: 45.9 us -> 44.1 us  [shards(): pl.pallas_call(kernel, out_shape=pltpu.VMEM(initial_states.shape, F32), i...]
where the time goes in v5:
time: 45.1 us; the launch traced here: 44.8 us
  Pallas kernels  44.1 us (98%)
  local copies, waits for them, and re-layouts  0.71 us (2%)
    pallas_call x1, Pallas kernels, shards(): pl.pallas_call(kernel, out_shape=pltpu.VMEM(initial_states.shape, F32), i...  44.1 us

profile of v5, /device:TPU:89, one launch (start us, length us, event | category | flops | bytes accessed | tf_op | source)
XLA Modules:
  0.0 44.8 jit_solution(322289077740392480)
XLA Ops:
  0.0 44.1 %shard_map.73 = f32[1,4,64,256]{3,2,1,0:T(8,128)S(1)} custom-call(f32[12]{0:T(128)} %cond.1, f32[12]{0:T(128)} %disp.1, f32[12]{0:T(128)} %fk.1, f32[12]{0:T(128)} %fn.1, f32[4,64]{1,0:T(4,128)} %load.1, f32[1,4,64,256]{3,2,1,0:T(8,128)} %init.1, s32[4,64,256]{2,1,0:T(8,128)} %mat.1), custom_call_target="tpu_custom_call" | custom-call | tf_op jit(solution)/shard_map/pallas_call | solution.py:744
  44.1 0.7 %copy.9 = f32[1,4,64,256]{3,2,1,0:T(8,128)} copy(f32[1,4,64,256]{3,2,1,0:T(8,128)S(1)} %shard_map.73) | data formatting | bytes 524288

commit v6 on v5

--- a/solution.py
+++ b/solution.py
@@ -13,7 +13,7 @@
 FY = 64
 CY = 32
 PAD = 8
-URGENT = 4
+URGENT = 3
 LAST = 7
 BREAK = 3
 LONGEST = max(BREAK, LAST - BREAK)
@@ -173,7 +173,7 @@
     def halo(item, s, arriving):
         src, dst = (
             (U.at[0, 3 + 3 * s, :, rows, :], U.at[0, 7 - 5 * s, :, rows, :]),
-            (M.at[2 + 3 * s + core * (1 - 2 * s)], M.at[6 - 5 * s + core * (1 - 2 * s)]),
+            (M.at[pl.ds(2 + 2 * s, 2)], M.at[pl.ds(6 - 6 * s, 2)]),
             (L.at[1], L.at[2 - 2 * s]),
             (U.at[0, 4 + s, :, rows, :], U.at[0, 8 - 7 * s, :, rows, :]),
             (GU.at[0, 3 - s, pl.ds(PAD, CY), :], GU.at[0, 5 - 5 * s, pl.ds(PAD, CY), :]),
@@ -190,11 +190,11 @@
             device_id_type=MESH,
         )
 
-    def to_sibling(s, arriving):
-        place = 6 - 5 * s + (1 - core if arriving else core) * (1 - 2 * s)
+    def to_sibling(s):
+        rows = pl.ds(6 - 6 * s, 2)
         return pltpu.make_async_remote_copy(
-            src_ref=M.at[place],
-            dst_ref=M.at[place],
+            src_ref=M.at[rows],
+            dst_ref=M.at[rows],
             send_sem=sib_send.at[s],
             recv_sem=sib_recv.at[s],
             device_id=device(sibling, t),
@@ -209,13 +209,20 @@
             @pl.when(jnp.logical_and(when, jnp.logical_and(sends[s], far[s])))
             def _():
                 for item in items:
-                    act(halo(item, s, False))
+                    if item == 1:
+
+                        @pl.when(core == 1)
+                        def _():
+                            act(halo(item, s, False))
+
+                    else:
+                        act(halo(item, s, False))
 
     def send_along(items, act):
         for item in items:
             for s in range(2):
 
-                @pl.when(jnp.logical_and(sends[s], jnp.logical_not(far[s])))
+                @pl.when(both(both(sends[s], jnp.logical_not(far[s])), jnp.logical_or(item != 1, core == 1)))
                 def _():
                     act(halo(item, s, False))
 
@@ -226,7 +233,7 @@
         for item in items:
             for s in range(2):
 
-                @pl.when(has[s])
+                @pl.when(both(has[s], jnp.logical_or(item != 1, core == 1)))
                 def _():
                     halo(item, s, True).wait_recv()
 
@@ -247,49 +254,7 @@
             U[i // 10, i % 10, h, pl.ds(PAD + FY, PAD), :] = zero
         return carry
 
-    lax.fori_loop(0, 50, blank_fine, 0)
-
-    def blank_coarse(i, carry):
-        for k in range(2):
-            W[k, i, pl.ds(0, PAD), :] = zero
-            W[k, i, pl.ds(PAD + CY, PAD), :] = zero
-        return carry
-
-    lax.fori_loop(0, 2 * SLOTS, blank_coarse, 0)
-    for k in range(2):
-        for r in range(6):
-            GU[k, r, pl.ds(0, PAD), :] = zero
-            GU[k, r, pl.ds(PAD + CY, PAD), :] = zero
-    for s in range(2):
-
-        @pl.when(jnp.logical_not(has[s]))
-        def _():
-            def clear(i, carry):
-                for h in range(2):
-                    U[i // 3, 7 - 7 * s + i % 3, h, pl.ds(PAD, FY), :] = jnp.zeros((FY, HALF), F32)
-                return carry
-
-            lax.fori_loop(0, 12, clear, 0)
-            for k in range(2):
-                for r in range(2):
-                    GU[k, 4 - 4 * s + r, pl.ds(PAD, CY), :] = jnp.zeros((CY, HALF), F32)
-
-    @pl.when(lead)
-    def _():
-        def clear(i, carry):
-            @pl.when(jnp.logical_not(inside(base + i - WIDE)))
-            def _():
-                for q in range(2):
-                    for f in range(6):
-                        CC[2 * i + q, f] = jnp.zeros((CY, HALF), F32)
-                    CL[2 * i + q] = jnp.zeros((CY, HALF), F32)
-                    W[0, 2 * i + q, pl.ds(PAD, CY), :] = jnp.zeros((CY, HALF), F32)
-                    for j in range(LONGEST):
-                        RD[j, 2 * i + q] = jnp.zeros((CY, HALF), F32)
-
-            return carry
-
-        lax.fori_loop(0, SLOTS, clear, 0)
+    lax.fori_loop(3, 7, blank_fine, 0)
 
     at = lane(8)
     tables = []
@@ -395,7 +360,7 @@
         look_up(r)
         return carry
 
-    lax.fori_loop(2, 6, own_rows, 0)
+    lax.fori_loop(3, 5, own_rows, 0)
 
     def inner_rows(r, carry):
         fine_step(0, r)
@@ -418,6 +383,52 @@
                 def _():
                     fine_step(k, r)
 
+    lax.fori_loop(0, 50, blank_fine, 0)
+
+    def blank_coarse(i, carry):
+        for k in range(2):
+            W[k, i, pl.ds(0, PAD), :] = zero
+            W[k, i, pl.ds(PAD + CY, PAD), :] = zero
+        return carry
+
+    lax.fori_loop(0, 2 * SLOTS, blank_coarse, 0)
+    for k in range(2):
+        for r in range(6):
+            GU[k, r, pl.ds(0, PAD), :] = zero
+            GU[k, r, pl.ds(PAD + CY, PAD), :] = zero
+    for s in range(2):
+
+        @pl.when(jnp.logical_not(has[s]))
+        def _():
+            def clear(i, carry):
+                for h in range(2):
+                    U[i // 3, 7 - 7 * s + i % 3, h, pl.ds(PAD, FY), :] = jnp.zeros((FY, HALF), F32)
+                return carry
+
+            lax.fori_loop(0, 12, clear, 0)
+            for k in range(2):
+                for r in range(2):
+                    GU[k, 4 - 4 * s + r, pl.ds(PAD, CY), :] = jnp.zeros((CY, HALF), F32)
+
+    @pl.when(lead)
+    def _():
+        def clear(i, carry):
+            @pl.when(jnp.logical_not(inside(base + i - WIDE)))
+            def _():
+                for q in range(2):
+                    for f in range(6):
+                        CC[2 * i + q, f] = jnp.zeros((CY, HALF), F32)
+                    CL[2 * i + q] = jnp.zeros((CY, HALF), F32)
+                    W[0, 2 * i + q, pl.ds(PAD, CY), :] = jnp.zeros((CY, HALF), F32)
+                    for j in range(LONGEST):
+                        RD[j, 2 * i + q] = jnp.zeros((CY, HALF), F32)
+
+            return carry
+
+        lax.fori_loop(0, SLOTS, clear, 0)
+
+    look_up(2)
+    look_up(5)
     for q in range(2):
         fields = mean_coefs(1 + q)
         for f in range(4):
@@ -476,18 +487,18 @@
     arrive((1,))
     for s in range(2):
 
-        @pl.when(has[s])
-        def _():
-            to_sibling(s, False).start()
+        @pl.when(both(has[s], core == 1))
+        def _():
+            to_sibling(s).start()
 
     arrive((2,))
 
     send_across(every[2:], jnp.logical_not(urgent), lambda copy: copy.start())
     for s in range(2):
 
-        @pl.when(has[s])
-        def _():
-            to_sibling(s, True).wait_recv()
+        @pl.when(both(has[s], core == 0))
+        def _():
+            to_sibling(s).wait_recv()
 
     for s in range(2):
 
@@ -504,7 +515,10 @@
     both_sides(0, 0)
     both_sides(1, 1)
     arrive((3,))
-    send_coefs(1, lambda copy: copy.start())
+    @pl.when(m > 1)
+    def _():
+        send_coefs(1, lambda copy: copy.start())
+
     both_sides(0, -1)
     both_sides(1, 0)
     both_sides(2, 1)
@@ -573,6 +587,11 @@
 
     each_block(lambda copy: copy.start())
 
+    @pl.when(m == 1)
+    def _():
+        send_coefs(1, lambda copy: copy.start())
+
+
     def carry_copy(pairs):
         to = base + 2 * pairs
         return pltpu.make_async_remote_copy(
@@ -618,9 +637,9 @@
     send_along(every, lambda copy: copy.wait_send())
     for s in range(2):
 
-        @pl.when(has[s])
-        def _():
-            to_sibling(s, False).wait_send()
+        @pl.when(both(has[s], core == 1))
+        def _():
+            to_sibling(s).wait_send()
     each_block(lambda copy: copy.wait_send())
     for e in range(2):
         send_coefs(e, lambda copy: copy.wait_send())

time: 45.1 us -> 44.1 us (0.978)
  Pallas kernels: 44.1 us -> 43.2 us
    pallas_call x1, Pallas kernels: 44.1 us -> 43.2 us  [shards(): pl.pallas_call(kernel, out_shape=pltpu.VMEM(initial_states.shape, F32), i...]
where the time goes in v6:
time: 44.1 us; the launch traced here: 43.9 us
  Pallas kernels  43.2 us (98%)
  local copies, waits for them, and re-layouts  0.71 us (2%)
    pallas_call x1, Pallas kernels, shards(): pl.pallas_call(kernel, out_shape=pltpu.VMEM(initial_states.shape, F32), i...  43.2 us

profile of v6, /device:TPU:89, one launch (start us, length us, event | category | flops | bytes accessed | tf_op | source)
XLA Modules:
  0.0 43.9 jit_solution(12239968920552456510)
XLA Ops:
  0.0 43.2 %shard_map.73 = f32[1,4,64,256]{3,2,1,0:T(8,128)S(1)} custom-call(f32[12]{0:T(128)} %cond.1, f32[12]{0:T(128)} %disp.1, f32[12]{0:T(128)} %fk.1, f32[12]{0:T(128)} %fn.1, f32[4,64]{1,0:T(4,128)} %load.1, f32[1,4,64,256]{3,2,1,0:T(8,128)} %init.1, s32[4,64,256]{2,1,0:T(8,128)} %mat.1), custom_call_target="tpu_custom_call" | custom-call | tf_op jit(solution)/shard_map/pallas_call | solution.py:763
  43.2 0.7 %copy.9 = f32[1,4,64,256]{3,2,1,0:T(8,128)} copy(f32[1,4,64,256]{3,2,1,0:T(8,128)S(1)} %shard_map.73) | data formatting | bytes 524288

commit v7 on v6

--- a/solution.py
+++ b/solution.py
@@ -484,6 +484,11 @@
 
     send_coefs(0, lambda copy: copy.start())
 
+    @pl.when(m == 6)
+    def _():
+        send_coefs(1, lambda copy: copy.start())
+
+
     arrive((1,))
     for s in range(2):
 
@@ -515,7 +520,7 @@
     both_sides(0, 0)
     both_sides(1, 1)
     arrive((3,))
-    @pl.when(m > 1)
+    @pl.when(m == 4)
     def _():
         send_coefs(1, lambda copy: copy.start())
 

time: 44.1 us -> 44.1 us (level)
  no operation moved by 1% of the time
where the time goes in v7:
time: 44.1 us; the launch traced here: 43.9 us
  Pallas kernels  43.2 us (98%)
  local copies, waits for them, and re-layouts  0.71 us (2%)
    pallas_call x1, Pallas kernels, shards(): pl.pallas_call(kernel, out_shape=pltpu.VMEM(initial_states.shape, F32), i...  43.2 us

profile of v7, /device:TPU:89, one launch (start us, length us, event | category | flops | bytes accessed | tf_op | source)
XLA Modules:
  0.0 43.9 jit_solution(10641414008791655493)
XLA Ops:
  0.0 43.2 %shard_map.73 = f32[1,4,64,256]{3,2,1,0:T(8,128)S(1)} custom-call(f32[12]{0:T(128)} %cond.1, f32[12]{0:T(128)} %disp.1, f32[12]{0:T(128)} %fk.1, f32[12]{0:T(128)} %fn.1, f32[4,64]{1,0:T(4,128)} %load.1, f32[1,4,64,256]{3,2,1,0:T(8,128)} %init.1, s32[4,64,256]{2,1,0:T(8,128)} %mat.1), custom_call_target="tpu_custom_call" | custom-call | tf_op jit(solution)/shard_map/pallas_call | solution.py:768
  43.2 0.7 %copy.9 = f32[1,4,64,256]{3,2,1,0:T(8,128)} copy(f32[1,4,64,256]{3,2,1,0:T(8,128)S(1)} %shard_map.73) | data formatting | bytes 524288

commit v8 on v7

--- a/solution.py
+++ b/solution.py
@@ -695,20 +695,23 @@
                 for q in range(rows):
                     W[1 - k, start + q, pl.ds(PAD, CY), :] = coarse_step(W, k, start + q, CC, CL, start + q)
 
-            def sweep(k, start):
-                def eight(i, carry):
-                    step(k, start + 8 * i, 8)
-                    return carry
-
-                lax.fori_loop(0, jnp.where(w == 3, 2, jnp.where(w == 0, 0, 1)), eight, 0)
+            def sweep(k, start, more):
+                tail = start + jnp.where(w >= 2, 8, 0)
+
+                @pl.when(w >= 2)
+                def _():
+                    step(k, start, 8)
 
                 @pl.when(jnp.logical_or(w == 0, w == 2))
                 def _():
-                    step(k, start + 4 * w, 4)
-
-            sweep(0, 2 * (WIDE - w) - 1)
-            step(0, 2 * (WIDE + w) + 3, 2)
-            sweep(1, 2 * (WIDE - w))
+                    step(k, tail, 4 + more)
+
+                @pl.when(jnp.logical_or(w == 1, w == 3))
+                def _():
+                    step(k, tail, 8 + more)
+
+            sweep(0, 2 * (WIDE - w) - 1, 2)
+            sweep(1, 2 * (WIDE - w), 0)
             for q in range(4):
                 GCB[j, q] = W[0, 2 * WIDE + q, pl.ds(PAD, CY), :]
             forwards(j, lambda copy: copy.start())

time: 44.1 us -> 44.1 us (level)
  no operation moved by 1% of the time
where the time goes in v8:
time: 44.1 us; the launch traced here: 43.9 us
  Pallas kernels  43.1 us (98%)
  local copies, waits for them, and re-layouts  0.71 us (2%)
    pallas_call x1, Pallas kernels, shards(): pl.pallas_call(kernel, out_shape=pltpu.VMEM(initial_states.shape, F32), i...  43.1 us

profile of v8, /device:TPU:89, one launch (start us, length us, event | category | flops | bytes accessed | tf_op | source)
XLA Modules:
  0.0 43.9 jit_solution(2374597925905927411)
XLA Ops:
  0.0 43.1 %shard_map.73 = f32[1,4,64,256]{3,2,1,0:T(8,128)S(1)} custom-call(f32[12]{0:T(128)} %cond.1, f32[12]{0:T(128)} %disp.1, f32[12]{0:T(128)} %fk.1, f32[12]{0:T(128)} %fn.1, f32[4,64]{1,0:T(4,128)} %load.1, f32[1,4,64,256]{3,2,1,0:T(8,128)} %init.1, s32[4,64,256]{2,1,0:T(8,128)} %mat.1), custom_call_target="tpu_custom_call" | custom-call | tf_op jit(solution)/shard_map/pallas_call | solution.py:771
  43.2 0.7 %copy.9 = f32[1,4,64,256]{3,2,1,0:T(8,128)} copy(f32[1,4,64,256]{3,2,1,0:T(8,128)S(1)} %shard_map.73) | data formatting | bytes 524288
